TPU v7x, 32 devices: a whole 2x2x4 slice. The times are simulated.
32 devices in a mesh: dp: 16 (over z, x, core), tensor: 2 (over y).
Axes of the slice: x: 2, y: 2, z: 4, core: 2. Of those that a mesh axis runs over, the one named last changes fastest.
Arguments:
- frames: bfloat16 [4096, 1536], P('dp', 'tensor'), may hold values from -6 to 6
- norm_gain: float32 [1536], replicated, may hold values from 0.5 to 2
- norm_bias: float32 [1536], replicated, may hold values from -3 to 3
- input_weight: bfloat16 [2, 1536, 1536], P(None, 'tensor'), may hold values from -0.15625 to 0.15625
- depth_weight: float32 [32, 1536], P(None, 'tensor'), may hold values from -1.5 to 1.5
- batch_scale: float32 [1536], P('tensor'), may hold values from 0.5 to 2
- batch_shift: float32 [1536], P('tensor'), may hold values from -3 to 3
- output_weight: bfloat16 [1536, 1536], P('tensor'), may hold values from -0.15625 to 0.15625
- upstream: bfloat16 [8192, 1536], P(('dp', 'tensor')), may hold values from -6 to 6
- replica_blocks: int32 [16], replicated, may hold values from 0 to 64, as said below
- segment: int32 [8192], P('dp'), may hold values from 0 to 32, as said below
Outputs:
- block_output: bfloat16 [8192, 1536], P(('dp', 'tensor'))
- frame_gradient: bfloat16 [4096, 1536], P('dp', 'tensor')
- input_weight_gradient: bfloat16 [2, 1536, 1536], P(None, 'tensor')
- output_weight_gradient: bfloat16 [1536, 1536], P('tensor')
- depth_weight_gradient: float32 [32, 1536], P(None, 'tensor')
- gain_gradient: float32 [1536], P('tensor')
- bias_gradient: float32 [1536], P('tensor')
Inputs may be any that keep to these rules, and one draw needn't show every extreme that they name: `replica_blocks`: the counts sum to 512. `segment`: within a replica's 512 slots the number starts at 0 and never falls.
All inputs are finite; a program needn't handle non-finite values.
Results may differ from a plain program's by a relative error of at most 0.017.
Values may be sent and summed in bfloat16 or wider, within the bound.
A program may use at most 128 MiB of HBM per device.

v0:
```python
import jax
import jax.numpy as jnp
from jax import lax
from jax.sharding import PartitionSpec as P

BLK = 8


epsilon = 1e-05


def routes(replica_blocks, replicas, my_index, load_blocks, cap_blocks, per_peer):
    run_ends = jnp.cumsum(replica_blocks)
    starts = run_ends - replica_blocks
    peer_ids = jnp.arange(replicas, dtype=jnp.int32)
    blocks = jnp.arange(load_blocks, dtype=jnp.int32)
    numbers = my_index + replicas * blocks
    target = jnp.sum((run_ends[None, :] <= numbers[:, None]).astype(jnp.int32), axis=1)
    target_start = jnp.sum(
        jnp.where(peer_ids[None, :] == target[:, None], starts[None, :], 0), axis=1
    )
    slot_out = blocks - (jnp.maximum(target_start - my_index, 0) + replicas - 1) // replicas
    is_mine = peer_ids == my_index
    my_start = jnp.sum(jnp.where(is_mine, starts, 0))
    my_end = jnp.sum(jnp.where(is_mine, run_ends, 0))
    bucket_pos = jnp.arange(per_peer, dtype=jnp.int32)
    skipped = (jnp.maximum(my_start - peer_ids, 0) + replicas - 1) // replicas
    arriving = peer_ids[:, None] + replicas * (skipped[:, None] + bucket_pos[None, :])
    filled = arriving < my_end
    landing = jnp.where(filled, arriving - my_start, cap_blocks)
    return (target, slot_out, landing, filled, my_end - my_start)


def on_device(
    frames,
    norm_gain,
    norm_bias,
    input_weight,
    depth_weight,
    batch_scale,
    batch_shift,
    output_weight,
    upstream,
    replica_blocks,
    segment,
):
    replicas = lax.axis_size("dp")
    my_index = lax.axis_index("dp")
    tensor_index = lax.axis_index("tensor")
    full_width = norm_gain.shape[0]
    load_rows, part_width = frames.shape
    row_count = segment.shape[0]
    rows_part = upstream.shape[0]
    kernel_taps = depth_weight.shape[0]
    load_blocks = load_rows // BLK
    cap_blocks = row_count // BLK
    per_peer = (cap_blocks + replicas - 1) // replicas
    target, slot_out, landing, filled, my_blocks = routes(
        replica_blocks, replicas, my_index, load_blocks, cap_blocks, per_peer
    )
    outbox = (
        jnp.zeros((replicas, per_peer, BLK, part_width), jnp.bfloat16)
        .at[target, slot_out]
        .set(frames.reshape(load_blocks, BLK, part_width))
    )
    arrived = lax.all_to_all(outbox, "dp", split_axis=0, concat_axis=0, tiled=True)
    packed = (
        jnp.zeros((cap_blocks, BLK, part_width), jnp.bfloat16)
        .at[landing.reshape(-1)]
        .set(arrived.reshape(-1, BLK, part_width), mode="drop")
    )
    local_rows = packed.reshape(row_count, part_width)
    active = jnp.arange(row_count, dtype=jnp.int32) // BLK < my_blocks
    row_start = tensor_index * rows_part
    active_mine = lax.dynamic_slice_in_dim(active, row_start, rows_part)[:, None]
    column_start = tensor_index * part_width
    gain_part = lax.dynamic_slice_in_dim(norm_gain, column_start, part_width)
    local_float = local_rows.astype(jnp.float32)
    gathered = lax.all_gather(local_rows, "tensor", axis=1, tiled=True)
    gathered_float = gathered.astype(jnp.float32)
    center = jnp.mean(gathered_float, axis=1, keepdims=True)
    spread = jnp.mean(jnp.square(gathered_float - center), axis=1, keepdims=True)
    scale_row = lax.rsqrt(spread + epsilon)
    normed = ((gathered_float - center) * scale_row * norm_gain + norm_bias).astype(jnp.bfloat16)
    residual_part = lax.dynamic_slice_in_dim(gathered, row_start, rows_part, 0)
    projected = jnp.einsum("td,kcd->ktc", normed, input_weight, preferred_element_type=jnp.float32)
    linear = projected[0]
    gate_sigmoid = jax.nn.sigmoid(projected[1])
    glu = (linear * gate_sigmoid).astype(jnp.bfloat16)
    front = kernel_taps // 2
    back = kernel_taps - 1 - front
    seg_pad = jnp.pad(segment, (front, back), constant_values=-1)
    active_pad = jnp.pad(active, (front, back))
    glu_pad = jnp.pad(glu, ((front, back), (0, 0)))
    tap_masks = []
    for offset in range(kernel_taps):
        same = (seg_pad[offset : offset + row_count] == segment) & active_pad[
            offset : offset + row_count
        ]
        tap_masks.append(same.astype(jnp.float32)[:, None])
    conv_sum = jnp.zeros((row_count, part_width), jnp.float32)
    for offset in range(kernel_taps):
        conv_sum = (
            conv_sum
            + depth_weight[offset]
            * glu_pad[offset : offset + row_count].astype(jnp.float32)
            * tap_masks[offset]
        )
    preswish = conv_sum * batch_scale + batch_shift
    pre_sigmoid = jax.nn.sigmoid(preswish)
    swish = (preswish * pre_sigmoid).astype(jnp.bfloat16)
    mixed_sum = lax.psum_scatter(
        jnp.dot(swish, output_weight, preferred_element_type=jnp.float32).astype(jnp.bfloat16),
        "tensor",
        scatter_dimension=0,
        tiled=True,
    ).astype(jnp.float32)
    block_output = jnp.where(
        active_mine, residual_part.astype(jnp.float32) + mixed_sum, 0.0
    ).astype(jnp.bfloat16)
    delta_piece = jnp.where(active_mine, upstream, jnp.zeros_like(upstream))
    delta_whole = lax.all_gather(delta_piece, "tensor", axis=0, tiled=True)
    delta_part = lax.dynamic_slice_in_dim(delta_whole, column_start, part_width, 1)
    delta_swish = lax.dot_general(
        delta_whole, output_weight, (((1,), (1,)), ((), ())), preferred_element_type=jnp.float32
    )
    out_local = lax.dot_general(
        swish, delta_whole, (((0,), (0,)), ((), ())), preferred_element_type=jnp.float32
    )
    delta_conv = delta_swish * pre_sigmoid * (1.0 + preswish * (1.0 - pre_sigmoid)) * batch_scale
    delta_pad = jnp.zeros((row_count + kernel_taps - 1, part_width), jnp.float32)
    tap_rows = []
    for offset in range(kernel_taps):
        contrib = delta_conv * tap_masks[offset]
        delta_pad = delta_pad.at[offset : offset + row_count].add(depth_weight[offset] * contrib)
        tap_rows.append(
            jnp.sum(contrib * glu_pad[offset : offset + row_count].astype(jnp.float32), axis=0)
        )
    delta_glu = delta_pad[front : front + row_count]
    tap_local = jnp.stack(tap_rows)
    delta_linear = (delta_glu * gate_sigmoid).astype(jnp.bfloat16)
    delta_gate = (delta_glu * linear * gate_sigmoid * (1.0 - gate_sigmoid)).astype(jnp.bfloat16)
    stacked = jnp.stack([delta_linear, delta_gate])
    weight_local = jnp.einsum("ktc,td->kcd", stacked, normed, preferred_element_type=jnp.float32)
    back_terms = jnp.einsum(
        "ktc,kcd->td", stacked, input_weight, preferred_element_type=jnp.float32
    )
    delta_normed = lax.psum_scatter(
        back_terms.astype(jnp.bfloat16), "tensor", scatter_dimension=1, tiled=True
    ).astype(jnp.float32)
    standard = (local_float - center) * scale_row
    gain_local = jnp.sum(delta_normed * standard, axis=0)
    bias_local = jnp.sum(delta_normed, axis=0)
    delta_standard = delta_normed * gain_part
    unit_total, cross_total = lax.psum(
        (jnp.sum(delta_standard, axis=1), jnp.sum(delta_standard * standard, axis=1)), "tensor"
    )
    delta_rows = delta_part.astype(jnp.float32) + scale_row * (
        delta_standard
        - (unit_total / full_width)[:, None]
        - standard * (cross_total / full_width)[:, None]
    )
    delta_blocks = delta_rows.astype(jnp.bfloat16).reshape(cap_blocks, BLK, part_width)
    homebound = jnp.where(
        filled[:, :, None, None],
        delta_blocks[jnp.minimum(landing, cap_blocks - 1)],
        jnp.zeros((), jnp.bfloat16),
    )
    returned = lax.all_to_all(homebound, "dp", split_axis=0, concat_axis=0, tiled=True)
    frame_gradient = returned[target, slot_out].reshape(load_rows, part_width)
    weight_summed, out_summed, tap_summed, gain_summed, bias_summed = lax.psum(
        (weight_local, out_local, tap_local, gain_local, bias_local), "dp"
    )
    return (
        block_output,
        frame_gradient,
        weight_summed.astype(jnp.bfloat16),
        out_summed.astype(jnp.bfloat16),
        tap_summed,
        gain_summed,
        bias_summed,
    )


def solution(mesh):
    in_specs = (
        P("dp", "tensor"),
        P(),
        P(),
        P(None, "tensor", None),
        P(None, "tensor"),
        P("tensor"),
        P("tensor"),
        P("tensor", None),
        P(("dp", "tensor"), None),
        P(),
        P("dp"),
    )
    out_specs = (
        P(("dp", "tensor"), None),
        P("dp", "tensor"),
        P(None, "tensor", None),
        P("tensor", None),
        P(None, "tensor"),
        P("tensor"),
        P("tensor"),
    )
    return jax.shard_map(
        on_device, mesh=mesh, in_specs=in_specs, out_specs=out_specs, check_vma=False
    )
```

profile of v0, /device:TPU:0, one launch (start us, length us, event | category | flops | bytes accessed | tf_op | source)
XLA Modules:
  0.0 726.1 jit_solution(5757926039595129058)
XLA Ops:
  10.7 5.1 scatter_fusion
  15.8 7.4 %all-to-all-start = ((bf16[16,4,8,768]{3,2,1,0:T(8,128)(2,1)}), bf16[16,4,8,768]{3,2,1,0:T(8,128)(2,1)S(1)}, u32[]{:S(2)}, u32[]{:S(2)}) async-start(bf16[16,4,8,768]{3,2,1,0:T(8,128)(2,1)} %scatter_fusion), calls=%async_computation | async-start | bytes 1572864 | tf_op jit(solution)/shard_map/all_to_all | solution.py:66
  25.4 16.5 %all-to-all-done = bf16[16,4,8,768]{3,2,1,0:T(8,128)(2,1)S(1)} async-done(((bf16[16,4,8,768]{3,2,1,0:T(8,128)(2,1)}), bf16[16,4,8,768]{3,2,1,0:T(8,128)(2,1)S(1)}, u32[]{:S(2)}, u32[]{:S(2)}) %all-to-all-start) | async-done | bytes 786464 | tf_op jit(solution)/shard_map/all_to_all | solution.py:66
  42.8 6.3 scatter_fusion.1
  54.4 23.8 %all-gather.3.cloned.1.call-done = bf16[512,1536]{1,0:T(8,128)(2,1)} async-done(((bf16[512,768]{1,0:T(8,128)(2,1)}), bf16[512,1536]{1,0:T(8,128)(2,1)}) %all-gather.3.cloned.1.call-update) | async-done | bytes 1572880 | tf_op jit(solution)/shard_map/all_gather | solution.py:79
  80.7 5.1 convolution_bitcast_fusion.1
  87.5 10.2 %fusion.93 = f32[512,768]{1,0:T(8,128)} fusion(bf16[512,768]{1,0:T(8,128)(2,1)S(1)} %multiply_convert_fusion.3, f32[768]{0:T(1024)S(1)} %copy-done.20, f32[768]{0:T(1024)S(1)} %copy-done.21, f32[512]{0:T(512)S(1)} %get-tuple-element.499, f32[768]{0:T(1024)S(1)} %get-tuple-element.457, f32[512]{0:T(512)S(1)} %get-tuple-element.500, ...), kind=kLoop, calls=%fused_computation.169 | loop fusion | flops 50724864 | bytes 2529280 | tf_op jit(solution)/shard_map/add | solution.py:109
  97.7 9.9 %all-gather.5.cloned.1.call-done = bf16[512,1536]{1,0:T(8,128)(2,1)} async-done(((bf16[256,1536]{1,0:T(8,128)(2,1)}), bf16[512,1536]{1,0:T(8,128)(2,1)}) %all-gather.5.cloned.1.call-update) | async-done | bytes 1572880 | tf_op jit(solution)/shard_map/all_gather | solution.py:122
  107.6 3.6 multiply_multiply_fusion.1
  114.1 5.0 scatter-add.109
  122.4 5.0 scatter-add.110
  130.6 5.0 scatter-add.111
  138.9 5.0 scatter-add.114
  147.2 5.0 scatter-add.115
  155.5 5.0 scatter-add.116
  163.8 5.0 scatter-add.119
  168.8 3.4 fusion.116
  175.0 5.0 scatter-add.121
  183.3 5.0 scatter-add.124
  191.6 5.0 scatter-add.125
  199.9 5.0 scatter-add.126
  208.2 5.0 scatter-add.129
  216.5 5.0 scatter-add.130
  224.8 5.1 scatter-add.131
  229.9 3.4 fusion.115
  236.2 5.0 scatter-add.135
  244.5 5.0 scatter-add.136
  252.8 5.0 scatter-add.139
  261.0 5.0 scatter-add.140
  269.3 5.0 scatter-add.141
  277.6 5.0 scatter-add.144
  285.9 5.0 scatter-add.145
  297.1 4.9 scatter-add.149
  302.1 3.8 fusion.96
  305.9 4.9 scatter-add.150
  314.2 4.9 scatter-add.151
  322.4 4.9 scatter-add.154
  330.7 4.9 scatter-add.155
  339.0 4.9 scatter-add.156
  347.2 4.9 scatter-add.159
  356.2 6.0 fusion.6
  364.6 4.0 convolution_convert_fusion
  368.7 3.9 fusion.106
  381.8 3.7 fusion.235
  385.5 5.6 fusion.121
  395.6 4.9 all-reduce.5
  406.3 5.7 all-to-all-start.1
  412.1 301.7 %all-reduce.10 = (bf16[2,768,1536]{2,1,0:T(8,128)(2,1)}, bf16[768,1536]{1,0:T(8,128)(2,1)}, f32[768]{0:T(1024)}, f32[768]{0:T(1024)}) all-reduce(f32[2,768,1536]{2,1,0:T(8,128)} %fusion.121, f32[768,1536]{1,0:T(8,128)} %fusion.235, f32[768]{0:T(1024)S(1)} %get-tuple-element.423, ...), channel_id=1, replica_groups=mesh['dp'=16,'tensor'=2] {'dp'}, use_global_device_ids=true, to_apply=%region_15.16 | all-reduce | flops 3540480 | bytes 21245952 | tf_op jit(solution)/shard_map/psum | solution.py:171
  (171 shorter events, 136.9 us)
Async XLA Ops:
  7.2 100.4 %copy-start = (bf16[768,1536]{1,0:T(8,128)(2,1)S(1)}, bf16[768,1536]{1,0:T(8,128)(2,1)}, u32[]{:S(2)}) copy-start(bf16[768,1536]{1,0:T(8,128)(2,1)} %param.82) | copy-start | bytes 7077892
  15.8 26.1 %all-to-all-start = ((bf16[16,4,8,768]{3,2,1,0:T(8,128)(2,1)}), bf16[16,4,8,768]{3,2,1,0:T(8,128)(2,1)S(1)}, u32[]{:S(2)}, u32[]{:S(2)}) async-start(bf16[16,4,8,768]{3,2,1,0:T(8,128)(2,1)} %scatter_fusion), calls=%async_computation | async-start | bytes 1572864 | tf_op jit(solution)/shard_map/all_to_all | solution.py:66
  23.2 55.0 %all-gather.3.cloned.1.call-start = ((), (), s32[]{:S(2)}) async-start(), calls=%async_computation.4 | async-start | bytes 2359296 | tf_op jit(solution)/shard_map/all_gather | solution.py:79
  41.9 0.9 copy-start.11
  49.1 0.9 copy-start.6
  49.1 4.6 copy-start.19
  49.2 4.9 copy-start.18
  50.0 57.5 %all-gather.5.cloned.1.call-start = ((), (), s32[]{:S(2)}) async-start(), calls=%async_computation.6 | async-start | bytes 2359296 | tf_op jit(solution)/shard_map/all_gather | solution.py:122
  53.6 340.0 %reduce-scatter.5.cloned.1.call-start = ((), (), s32[]{:S(2)}) async-start(), calls=%async_computation.7 | async-start | bytes 2359296 | tf_op jit(solution)/shard_map/reduce_scatter | solution.py:148
  78.2 1.9 copy-start.9
  78.2 2.4 copy-start.22
  78.2 2.4 copy-start.23
  85.8 1.7 copy-start.8
  85.8 1.7 copy-start.20
  85.8 1.6 copy-start.21
  111.2 1.6 copy-start.1
  168.8 3.4 copy-start.2
  229.9 3.4 copy-start.3
  290.9 3.4 copy-start.4
  355.1 0.9 copy-start.13
  355.1 1.1 copy-start.15
  362.3 351.4 %reduce-scatter.3.cloned.1.call-start = ((), (), s32[]{:S(2)}) async-start(), calls=%async_computation.5 | async-start | bytes 2359296 | tf_op jit(solution)/shard_map/reduce_scatter | solution.py:112
  368.7 348.9 %all-reduce.9.cloned.1.call-start = ((), (), s32[]{:S(2)}) async-start(), calls=%async_computation.8 | async-start | bytes 196608 | tf_op jit(solution)/shard_map/psum | solution.py:171
  368.7 4.0 copy-start.5
  377.3 4.4 copy-start.17
  379.5 2.2 copy-start.12
  381.7 3.7 copy-start.10
  381.7 3.7 copy-start.14
  381.8 3.7 copy-start.16
  385.5 8.2 %copy-start.7 = (bf16[64,8,768]{2,1,0:T(8,128)(2,1)S(1)}, bf16[64,8,768]{2,1,0:T(8,128)(2,1)}, u32[]{:S(2)}) copy-start(bf16[64,8,768]{2,1,0:T(8,128)(2,1)} %copy-done.6) | copy-start | bytes 2359300
  406.3 309.9 %all-to-all-start.1 = ((bf16[16,4,8,768]{3,2,1,0:T(8,128)(2,1)}), bf16[16,4,8,768]{3,2,1,0:T(8,128)(2,1)S(1)}, u32[]{:S(2)}, u32[]{:S(2)}) async-start(bf16[16,4,8,768]{3,2,1,0:T(8,128)(2,1)} %broadcast_select_fusion.1), calls=%async_computation.3 | async-start | bytes 1572864 | tf_op jit(solution)/shard_map/all_to_all | solution.py:169
Sparse Core Ops, SparseCore 0:
  50.2 27.9 all-gather.2
  80.3 27.2 all-gather.4
  362.4 26.0 reduce-scatter.4
  390.7 26.1 reduce-scatter.2
  420.8 118.4 all-reduce.8
where the time goes:
time: 740 us; the launch traced here: 726 us
  blocking collectives  307 us (41%)
  local copies, waits for them, and re-layouts  166 us (22%)
  other arithmetic  146 us (20%)
  waiting for transfers between devices  50.3 us (7%)
  matrix products  28 us (4%)
  between operations  16.2 us (2%)
  starting transfers between devices  13.3 us (2%)
    psum x1, blocking collectives, on_device(): lax.psum((weight_local, out_local, tap_local, gain_local, bias_local), 'dp')  302 us
    scatter-add x29, local copies, waits for them, and re-layouts, on_device(): delta_pad.at[offset:offset + row_count].add(depth_weight[offset] * contrib)  140 us
    add x27, other arithmetic, on_device(): delta_pad.at[offset:offset + row_count].add(depth_weight[offset] * contrib)  86.7 us
    all_gather x1, waiting for transfers between devices, on_device(): gathered = lax.all_gather(local_rows, 'tensor', axis=1, tiled=True)  23.8 us
    all_to_all x1, waiting for transfers between devices, on_device(): lax.all_to_all(outbox, 'dp', split_axis=0, concat_axis=0, tiled=True)  16.5 us
    reduce_sum x6, other arithmetic, on_device(): jnp.sum(contrib * glu_pad[offset:offset + row_count].astype(jnp.float32),...  16.4 us
  transfers between devices with their start and end apart: 7, of which 3 were waited for; matrix products, arithmetic and copies ran while one was open for 9% of the time, Pallas kernels for 0%

commit v1 on v0

v1 whole, which is shorter than its diff:
```python
import functools

import jax
import jax.numpy as jnp
from jax import lax
from jax.experimental import pallas as pl
from jax.experimental.pallas import tpu as pltpu
from jax.sharding import PartitionSpec as P

BLK = 8


epsilon = 1e-05


def cdiv(a, b):
    return (a + b - 1) // b


def conv_kernel(
    taps,
    front,
    tile,
    linear_ref,
    gate_ref,
    delta_ref,
    seg_ref,
    active_ref,
    weight_ref,
    scale_ref,
    shift_ref,
    swish_ref,
    dlin_ref,
    dgate_ref,
    tap_ref,
    glu_pad,
    conv_pad,
    seg_pad,
    tap_acc,
):
    rows, width = linear_ref.shape
    pad = taps
    padded = rows + 2 * pad

    zeros = jnp.zeros((pad, width), jnp.float32)
    glu_pad[0:pad, :] = zeros
    glu_pad[pad + rows : padded, :] = zeros
    conv_pad[0:pad, :] = zeros
    conv_pad[pad + rows : padded, :] = zeros

    @pl.when(pl.program_id(0) == 0)
    def _():
        outside = jnp.full((pad, width), -1, jnp.int32)
        seg_pad[0:pad, :] = outside
        seg_pad[pad + rows : padded, :] = outside
        seg_pad[pad : pad + rows, :] = jnp.broadcast_to(seg_ref[...], (rows, width))

    tap_acc[...] = jnp.zeros_like(tap_acc)

    for start in range(0, rows, tile):
        part = pl.ds(start, tile)
        glu = linear_ref[part, :] * jax.nn.sigmoid(gate_ref[part, :])
        glu = glu.astype(jnp.bfloat16).astype(jnp.float32)
        glu_pad[pl.ds(pad + start, tile), :] = jnp.where(active_ref[part, :] > 0, glu, 0.0)

    @pl.loop(0, rows // tile)
    def _(step):
        start = pl.multiple_of(step * tile, tile)
        part = pl.ds(start, tile)
        own = seg_pad[pl.ds(pad + start, tile), :]
        total = jnp.zeros((tile, width), jnp.float32)
        for j in range(taps):
            near = pl.ds(start + (pad + j - front), tile)
            picked = jnp.where(seg_pad[near, :] == own, glu_pad[near, :], 0.0)
            total = total + weight_ref[j : j + 1, :] * picked
        scale = scale_ref[...]
        preswish = total * scale + shift_ref[...]
        pre_sigmoid = jax.nn.sigmoid(preswish)
        swish_ref[part, :] = (preswish * pre_sigmoid).astype(jnp.bfloat16)
        conv_pad[pl.ds(pad + start, tile), :] = (
            delta_ref[part, :]
            * pre_sigmoid
            * (1.0 + preswish * (1.0 - pre_sigmoid))
            * scale
        )

    @pl.loop(0, rows // tile)
    def _(step):
        start = pl.multiple_of(step * tile, tile)
        part = pl.ds(start, tile)
        own = seg_pad[pl.ds(pad + start, tile), :]
        glu = glu_pad[pl.ds(pad + start, tile), :]
        total = jnp.zeros((tile, width), jnp.float32)
        for j in range(taps):
            near = pl.ds(start + (pad + front - j), tile)
            picked = jnp.where(seg_pad[near, :] == own, conv_pad[near, :], 0.0)
            total = total + weight_ref[j : j + 1, :] * picked
            product = (glu * picked).reshape(tile // 8, 8, width)
            tap_acc[j] = tap_acc[j] + jnp.sum(product, axis=0)
        total = jnp.where(active_ref[part, :] > 0, total, 0.0)
        gate_sigmoid = jax.nn.sigmoid(gate_ref[part, :])
        dlin = total * gate_sigmoid
        dlin_ref[part, :] = dlin.astype(jnp.bfloat16)
        dgate_ref[part, :] = (dlin * linear_ref[part, :] * (1.0 - gate_sigmoid)).astype(
            jnp.bfloat16
        )

    tap_ref[...] = jnp.sum(tap_acc[...], axis=1)


def conv_both(projected, delta_swish, segment, active, weight, scale, shift):
    _, rows, given = projected.shape
    taps = weight.shape[0]
    width = 128
    channels = cdiv(given, width) * width

    def widen(array):
        extra = channels - given
        return jnp.pad(array, [(0, 0)] * (array.ndim - 1) + [(0, extra)]) if extra else array

    projected, delta_swish, weight = widen(projected), widen(delta_swish), widen(weight)
    scale, shift = widen(scale), widen(shift)
    tile = min(64, rows)
    padded = rows + 2 * taps
    column = pl.BlockSpec((rows, width), lambda c: (0, c))
    half = lambda h: pl.BlockSpec((None, rows, width), lambda c: (h, 0, c))
    row = pl.BlockSpec((1, width), lambda c: (0, c))
    whole = pl.BlockSpec((rows, 1), lambda c: (0, 0))
    results = pl.pallas_call(
        functools.partial(conv_kernel, taps, taps // 2, tile),
        grid=(channels // width,),
        out_shape=(
            jax.ShapeDtypeStruct((rows, channels), jnp.bfloat16),
            jax.ShapeDtypeStruct((rows, channels), jnp.bfloat16),
            jax.ShapeDtypeStruct((rows, channels), jnp.bfloat16),
            jax.ShapeDtypeStruct((taps, channels), jnp.float32),
        ),
        in_specs=[
            half(0),
            half(1),
            column,
            whole,
            whole,
            pl.BlockSpec((taps, width), lambda c: (0, c)),
            row,
            row,
        ],
        out_specs=[column, column, column, pl.BlockSpec((taps, width), lambda c: (0, c))],
        scratch_shapes=[
            pltpu.VMEM((padded, width), jnp.float32),
            pltpu.VMEM((padded, width), jnp.float32),
            pltpu.VMEM((padded, width), jnp.int32),
            pltpu.VMEM((taps, 8, width), jnp.float32),
        ],
        compiler_params=pltpu.CompilerParams(vmem_limit_bytes=24 * 1024 * 1024),
        cost_estimate=pl.CostEstimate(
            flops=10 * rows * channels * taps,
            bytes_accessed=18 * rows * channels,
            transcendentals=3 * rows * channels,
        ),
    )(
        projected,
        projected,
        delta_swish,
        segment[:, None],
        active.astype(jnp.int32)[:, None],
        weight,
        scale[None, :],
        shift[None, :],
    )
    return [result[:, :given] for result in results] if channels != given else results


def on_device(
    frames,
    norm_gain,
    norm_bias,
    input_weight,
    depth_weight,
    batch_scale,
    batch_shift,
    output_weight,
    upstream,
    replica_blocks,
    segment,
):
    replicas = lax.axis_size("dp")
    my_index = lax.axis_index("dp")
    tensor_index = lax.axis_index("tensor")
    full_width = norm_gain.shape[0]
    load_rows, part_width = frames.shape
    row_count = segment.shape[0]
    rows_part = upstream.shape[0]
    load_blocks = load_rows // BLK
    cap_blocks = row_count // BLK
    per_peer = cdiv(cap_blocks, replicas)
    row_start = tensor_index * rows_part
    column_start = tensor_index * part_width

    run_ends = jnp.cumsum(replica_blocks)
    starts = run_ends - replica_blocks
    peers = jnp.arange(replicas, dtype=jnp.int32)
    is_mine = peers == my_index
    my_start = jnp.sum(jnp.where(is_mine, starts, 0))
    my_blocks = jnp.sum(jnp.where(is_mine, replica_blocks, 0))
    my_end = my_start + my_blocks
    bucket = jnp.arange(per_peer, dtype=jnp.int32)
    first_out = cdiv(jnp.maximum(starts - my_index, 0), replicas)
    send_block = jnp.minimum(first_out[:, None] + bucket[None, :], load_blocks - 1)
    skipped = cdiv(jnp.maximum(my_start - peers, 0), replicas)
    arriving = peers[:, None] + replicas * (skipped[:, None] + bucket[None, :])
    landing = jnp.clip(arriving - my_start, 0, cap_blocks - 1)
    slots = jnp.arange(cap_blocks, dtype=jnp.int32)
    slot_number = my_start + slots
    slot_source = slot_number % replicas
    slot_skipped = cdiv(jnp.maximum(my_start - slot_source, 0), replicas)
    slot_pos = jnp.clip(slot_number // replicas - slot_skipped, 0, per_peer - 1)
    pick_in = slot_source * per_peer + slot_pos
    load_numbers = my_index + replicas * jnp.arange(load_blocks, dtype=jnp.int32)
    target = jnp.sum((run_ends[None, :] <= load_numbers[:, None]).astype(jnp.int32), axis=1)
    target_start = jnp.sum(jnp.where(peers[None, :] == target[:, None], starts[None, :], 0), axis=1)
    slot_out = jnp.arange(load_blocks, dtype=jnp.int32) - cdiv(
        jnp.maximum(target_start - my_index, 0), replicas
    )
    pick_back = target * per_peer + slot_out

    active = slots < my_blocks
    active_rows = jnp.repeat(active, BLK)
    active_mine = lax.dynamic_slice_in_dim(active_rows, row_start, rows_part)[:, None]

    delta_piece = jnp.where(active_mine, upstream, jnp.zeros_like(upstream))
    delta_whole = lax.all_gather(delta_piece, "tensor", axis=0, tiled=True)

    outbox = frames.reshape(load_blocks, BLK, part_width)[send_block.reshape(-1)]
    arrived = lax.all_to_all(
        outbox.reshape(replicas, per_peer, BLK, part_width),
        "dp",
        split_axis=0,
        concat_axis=0,
        tiled=True,
    )
    packed = jnp.where(
        active[:, None, None],
        arrived.reshape(replicas * per_peer, BLK, part_width)[pick_in],
        jnp.zeros((), jnp.bfloat16),
    )
    local_rows = packed.reshape(row_count, part_width)
    gathered = lax.all_gather(local_rows, "tensor", axis=1, tiled=True)

    delta_swish = lax.dot_general(
        delta_whole, output_weight, (((1,), (1,)), ((), ())), preferred_element_type=jnp.float32
    )

    gathered_float = gathered.astype(jnp.float32)
    center = jnp.mean(gathered_float, axis=1, keepdims=True)
    spread = jnp.mean(jnp.square(gathered_float - center), axis=1, keepdims=True)
    scale_row = lax.rsqrt(spread + epsilon)
    standard_full = (gathered_float - center) * scale_row
    normed = (standard_full * norm_gain + norm_bias).astype(jnp.bfloat16)
    projected = jnp.einsum("td,kcd->ktc", normed, input_weight, preferred_element_type=jnp.float32)

    swish, delta_linear, delta_gate, tap_local = conv_both(
        projected, delta_swish, segment, active_rows, depth_weight, batch_scale, batch_shift
    )

    back_term = (
        jnp.dot(delta_linear, input_weight[0], preferred_element_type=jnp.float32)
        + jnp.dot(delta_gate, input_weight[1], preferred_element_type=jnp.float32)
    ).astype(jnp.bfloat16)
    delta_normed = lax.psum_scatter(back_term, "tensor", scatter_dimension=1, tiled=True).astype(
        jnp.float32
    )
    back_float = back_term.astype(jnp.float32)
    back_standard = back_float * standard_full
    unit_local = jnp.sum(back_float * norm_gain, axis=1)
    cross_local = jnp.sum(back_standard * norm_gain, axis=1)
    unit_total, cross_total = lax.psum((unit_local, cross_local), "tensor")
    norm_sums = lax.psum(
        jnp.stack([jnp.sum(back_standard, axis=0), jnp.sum(back_float, axis=0)]), ("dp", "tensor")
    )
    norm_part = lax.dynamic_slice_in_dim(norm_sums, column_start, part_width, 1)

    mixed_sum = lax.psum_scatter(
        jnp.dot(swish, output_weight, preferred_element_type=jnp.float32).astype(jnp.bfloat16),
        "tensor",
        scatter_dimension=0,
        tiled=True,
    ).astype(jnp.float32)
    residual_part = lax.dynamic_slice_in_dim(gathered, row_start, rows_part, 0)
    block_output = jnp.where(
        active_mine, residual_part.astype(jnp.float32) + mixed_sum, 0.0
    ).astype(jnp.bfloat16)

    def over_rows(left, right):
        return lax.dot_general(
            left, right, (((0,), (0,)), ((), ())), preferred_element_type=jnp.float32
        ).astype(jnp.bfloat16)

    def summed(term):
        piece = lax.psum_scatter(term, "dp", scatter_dimension=0, tiled=True)
        return lax.all_gather(piece, "dp", axis=0, tiled=True)

    out_summed = summed(over_rows(swish, delta_whole))
    linear_summed = summed(over_rows(delta_linear, normed))
    gate_summed = summed(over_rows(delta_gate, normed))
    tap_summed = lax.psum(tap_local, "dp")

    gain_part = lax.dynamic_slice_in_dim(norm_gain, column_start, part_width)
    standard = (local_rows.astype(jnp.float32) - center) * scale_row
    delta_part = lax.dynamic_slice_in_dim(delta_whole, column_start, part_width, 1)
    delta_rows = delta_part.astype(jnp.float32) + scale_row * (
        delta_normed * gain_part
        - (unit_total / full_width)[:, None]
        - standard * (cross_total / full_width)[:, None]
    )
    delta_blocks = delta_rows.astype(jnp.bfloat16).reshape(cap_blocks, BLK, part_width)
    homebound = delta_blocks[landing.reshape(-1)].reshape(replicas, per_peer, BLK, part_width)
    returned = lax.all_to_all(homebound, "dp", split_axis=0, concat_axis=0, tiled=True)
    frame_gradient = returned.reshape(replicas * per_peer, BLK, part_width)[pick_back].reshape(
        load_rows, part_width
    )
    return (
        block_output,
        frame_gradient,
        jnp.stack([linear_summed, gate_summed]),
        out_summed,
        tap_summed,
        norm_part[0],
        norm_part[1],
    )


def solution(mesh):
    in_specs = (
        P("dp", "tensor"),
        P(),
        P(),
        P(None, "tensor", None),
        P(None, "tensor"),
        P("tensor"),
        P("tensor"),
        P("tensor", None),
        P(("dp", "tensor"), None),
        P(),
        P("dp"),
    )
    out_specs = (
        P(("dp", "tensor"), None),
        P("dp", "tensor"),
        P(None, "tensor", None),
        P("tensor", None),
        P(None, "tensor"),
        P("tensor"),
        P("tensor"),
    )
    return jax.shard_map(
        on_device, mesh=mesh, in_specs=in_specs, out_specs=out_specs, check_vma=False
    )
```

time: 740 us -> 601 us (0.81); the launches traced: 726 us -> 600 us
  waiting for transfers between devices: 50.3 us -> 434 us
  blocking collectives: 307 us -> 45.4 us
  local copies, waits for them, and re-layouts: 166 us -> 20.3 us
  other arithmetic: 146 us -> 20.6 us
  Pallas kernels: 0 us -> 20.7 us
    psum x2, blocking collectives: 307 us -> 45.4 us  [the longest x1 40.4 us: on_device(): lax.psum(jnp.stack([jnp.sum(back_standard, axis=0), jnp.sum(back_float, a...]
    reduce_scatter x1 -> x4, waiting for transfers between devices: 0.02 us -> 194 us  [the longest x3 173 us: summed(): piece = lax.psum_scatter(term, 'dp', scatter_dimension=0, tiled=True)]
    scatter-add x29 -> x0, local copies, waits for them, and re-layouts: 140 us -> none  [on_device(): delta_pad.at[offset:offset + row_count].add(depth_weight[offset] * contrib)]
    all_gather x0 -> x3, waiting for transfers between devices: none -> 99.2 us  [summed(): return lax.all_gather(piece, 'dp', axis=0, tiled=True)]
    add x29 -> x1, other arithmetic: 96.9 us -> 0.01 us  [on_device(): my_index + replicas * jnp.arange(load_blocks, dtype=jnp.int32)]
    psum x1, waiting for transfers between devices: 0.01 us -> 90.3 us  [on_device(): tap_summed = lax.psum(tap_local, 'dp')]
    pallas_call x0 -> x1, Pallas kernels: none -> 20.7 us  [conv_both(): pl.pallas_call(functools.partial(conv_kernel, taps, taps // 2, tile), gri...]
    reduce_sum x10 -> x3, other arithmetic: 19.8 us -> 1.48 us  [the longest x1 1.3 us: on_device(): my_start = jnp.sum(jnp.where(is_mine, starts, 0))]
  transfers between devices with their start and end apart: 7 -> 13, of which waited for: 3 -> 11; matrix products, arithmetic and copies ran while one was open for 9% -> 8% of each run, Pallas kernels for 0% -> 0%
where the time goes in v1:
time: 601 us; the launch traced here: 600 us
  waiting for transfers between devices  434 us (72%)
  blocking collectives  45.4 us (8%)
  matrix products  31.6 us (5%)
  Pallas kernels  20.7 us (3%)
  other arithmetic  20.6 us (3%)
  local copies, waits for them, and re-layouts  20.3 us (3%)
  between operations  14.2 us (2%)
  starting transfers between devices  13.6 us (2%)
    reduce_scatter x3, waiting for transfers between devices, summed(): piece = lax.psum_scatter(term, 'dp', scatter_dimension=0, tiled=True)  173 us
    all_gather x3, waiting for transfers between devices, summed(): return lax.all_gather(piece, 'dp', axis=0, tiled=True)  99.2 us
    psum x1, waiting for transfers between devices, on_device(): tap_summed = lax.psum(tap_local, 'dp')  90.3 us
    psum x1, blocking collectives, on_device(): lax.psum(jnp.stack([jnp.sum(back_standard, axis=0), jnp.sum(back_float, a...  40.4 us
    all_gather x1, waiting for transfers between devices, on_device(): gathered = lax.all_gather(local_rows, 'tensor', axis=1, tiled=True)  25.4 us
    reduce_scatter x1, waiting for transfers between devices, on_device(): lax.psum_scatter(back_term, 'tensor', scatter_dimension=1, tiled=True)  21.4 us
    pallas_call x1, Pallas kernels, conv_both(): pl.pallas_call(functools.partial(conv_kernel, taps, taps // 2, tile), gri...  20.7 us
    all_to_all x1, waiting for transfers between devices, on_device(): lax.all_to_all(outbox.reshape(replicas, per_peer, BLK, part_width), 'dp',...  14.8 us
  transfers between devices with their start and end apart: 13, of which 11 were waited for; matrix products, arithmetic and copies ran while one was open for 8% of the time, Pallas kernels for 0%

profile of v1, /device:TPU:0, one launch (start us, length us, event | category | flops | bytes accessed | tf_op | source)
XLA Modules:
  0.0 600.0 jit_solution(4948693554838521088)
XLA Ops:
  7.2 0.9 copy.22
  8.2 1.3 fusion.17
  9.5 0.7 and_select_fusion.1
  10.4 2.5 gather_fusion
  12.9 7.4 %all-to-all-start = ((bf16[16,4,8,768]{3,2,1,0:T(8,128)(2,1)}), bf16[16,4,8,768]{3,2,1,0:T(8,128)(2,1)S(1)}, u32[]{:S(2)}, u32[]{:S(2)}) async-start(bf16[16,4,8,768]{3,2,1,0:T(8,128)(2,1)} %bitcast.63), calls=%async_computation | async-start | bytes 1572864 | tf_op jit(solution)/shard_map/all_to_all | solution.py:235
  20.3 0.7 iota_compare_fusion.1
  21.2 2.1 broadcast_select_fusion
  23.4 0.7 fusion.19
  24.1 14.8 %all-to-all-done = bf16[16,4,8,768]{3,2,1,0:T(8,128)(2,1)S(1)} async-done(((bf16[16,4,8,768]{3,2,1,0:T(8,128)(2,1)}), bf16[16,4,8,768]{3,2,1,0:T(8,128)(2,1)S(1)}, u32[]{:S(2)}, u32[]{:S(2)}) %all-to-all-start) | async-done | bytes 786464 | tf_op jit(solution)/shard_map/all_to_all | solution.py:235
  38.9 0.9 copy-done.13
  39.8 1.7 gather_fusion.1
  41.6 1.1 bitcast_select_fusion
  43.2 8.9 %all-gather.8.cloned.1.call-done = bf16[512,1536]{1,0:T(8,128)(2,1)} async-done(((bf16[256,1536]{1,0:T(8,128)(2,1)}), bf16[512,1536]{1,0:T(8,128)(2,1)}) %all-gather.8.cloned.1.call-update) | async-done | bytes 1572880 | tf_op jit(solution)/shard_map/all_gather | solution.py:232
  52.1 4.0 fusion.26.delta_ref
  56.0 25.4 %all-gather.6.cloned.1.call-done = bf16[512,1536]{1,0:T(8,128)(2,1)} async-done(((bf16[512,768]{1,0:T(8,128)(2,1)}), bf16[512,1536]{1,0:T(8,128)(2,1)}) %all-gather.6.cloned.1.call-update) | async-done | bytes 1572880 | tf_op jit(solution)/shard_map/all_gather | solution.py:248
  81.4 1.8 convert_reduce_fusion.1
  83.9 5.0 convolution_bitcast_fusion.linear_ref.gate_ref
  89.0 20.7 %shard_map.162 = (bf16[512,768]{1,0:T(8,128)(2,1)S(1)}, bf16[512,768]{1,0:T(8,128)(2,1)S(1)}, bf16[512,768]{1,0:T(8,128)(2,1)S(1)}, f32[32,768]{1,0:T(8,128)}) custom-call(f32[2,512,768]{2,1,0:T(8,128)S(1)} %convolution_bitcast_fusion.linear_ref.gate_ref, f32[2,512,768]{2,1,0:T(8,128)S(1)} %convolution_bitcast_fusion.linear_ref.gate_ref, ...), custom_call_target="tpu_custom_call" | custom-call | flops 125829120 | bytes 7077888 | tf_op jit(solution)/shard_map/pallas_call | solution.py:129
  109.7 0.9 copy-done.3
  110.6 0.9 copy-done.7
  111.5 0.9 copy-done.5
  112.4 3.0 convolution_convert_fusion.1
  115.5 1.1 copy-done.8
  116.5 4.4 convolution_convert_fusion.2
  121.0 1.1 copy-done.4
  122.0 4.3 convolution_convert_fusion
  126.5 3.5 fusion.10
  130.0 4.8 fusion.8
  134.9 2.5 convolution_convert_fusion.3
  137.7 40.8 %reduce-scatter.12.cloned.1.call-done = bf16[48,1536]{1,0:T(8,128)(2,1)} async-done(((bf16[768,1536]{1,0:T(8,128)(2,1)}), bf16[48,1536]{1,0:T(8,128)(2,1)}) %reduce-scatter.12.cloned.1.call-update) | async-done | bytes 147472 | tf_op jit(solution)/shard_map/reduce_scatter | solution.py:300
  178.6 66.7 %reduce-scatter.10.cloned.1.call-done = bf16[48,1536]{1,0:T(8,128)(2,1)} async-done(((bf16[768,1536]{1,0:T(8,128)(2,1)}), bf16[48,1536]{1,0:T(8,128)(2,1)}) %reduce-scatter.10.cloned.1.call-update) | async-done | bytes 147472 | tf_op jit(solution)/shard_map/reduce_scatter | solution.py:300
  245.3 65.6 %reduce-scatter.14.cloned.1.call-done = bf16[48,1536]{1,0:T(8,128)(2,1)} async-done(((bf16[768,1536]{1,0:T(8,128)(2,1)}), bf16[48,1536]{1,0:T(8,128)(2,1)}) %reduce-scatter.14.cloned.1.call-update) | async-done | bytes 147472 | tf_op jit(solution)/shard_map/reduce_scatter | solution.py:300
  311.0 0.7 subtract_clamp_fusion
  311.8 4.9 all-reduce
  316.8 21.4 %reduce-scatter.8.cloned.1.call-done = bf16[512,768]{1,0:T(8,128)(2,1)} async-done(((bf16[512,1536]{1,0:T(8,128)(2,1)}), bf16[512,768]{1,0:T(8,128)(2,1)}) %reduce-scatter.8.cloned.1.call-update) | async-done | bytes 786448 | tf_op jit(solution)/shard_map/reduce_scatter | solution.py:270
  338.2 3.0 fusion.15
  341.2 2.6 gather_fusion.2
  343.8 5.6 all-to-all-start.1
  350.1 40.4 %psum.31 = f32[2,1536]{1,0:T(2,128)S(1)} all-reduce(f32[2,1536]{1,0:T(2,128)S(1)} %pad_maximum_fusion.1), channel_id=1, replica_groups=mesh['dp'=16,'tensor'=2] {'dp','tensor'}, use_global_device_ids=true, to_apply=%region_19.20 | all-reduce | flops 3072 | bytes 24576 | tf_op jit(solution)/shard_map/psum | solution.py:278
  390.6 0.7 dynamic-slice_reduce_fusion
  391.3 2.5 select_convert_fusion
  393.8 1.3 gather_fusion.3
  395.1 17.0 %all-gather.12.cloned.1.call-done = bf16[768,1536]{1,0:T(8,128)(2,1)} async-done(((bf16[48,1536]{1,0:T(8,128)(2,1)}), bf16[768,1536]{1,0:T(8,128)(2,1)}) %all-gather.12.cloned.1.call-update) | async-done | bytes 2359312 | tf_op jit(solution)/shard_map/all_gather | solution.py:301
  412.1 43.7 %all-gather.10.cloned.1.call-done = bf16[768,1536]{1,0:T(8,128)(2,1)} async-done(((bf16[48,1536]{1,0:T(8,128)(2,1)}), bf16[768,1536]{1,0:T(8,128)(2,1)}) %all-gather.10.cloned.1.call-update) | async-done | bytes 2359312 | tf_op jit(solution)/shard_map/all_gather | solution.py:301
  455.8 5.0 pad_maximum_fusion
  460.8 38.5 %all-gather.14.cloned.1.call-done = bf16[768,1536]{1,0:T(8,128)(2,1)} async-done(((bf16[48,1536]{1,0:T(8,128)(2,1)}), bf16[768,1536]{1,0:T(8,128)(2,1)}) %all-gather.14.cloned.1.call-update) | async-done | bytes 2359312 | tf_op jit(solution)/shard_map/all_gather | solution.py:301
  499.3 90.3 %all-reduce.3.cloned.1.call-done = f32[32,768]{1,0:T(8,128)} async-done(((f32[32,768]{1,0:T(8,128)}), f32[32,768]{1,0:T(8,128)}) %all-reduce.3.cloned.1.call-update) | async-done | bytes 98320 | tf_op jit(solution)/shard_map/psum | solution.py:306
  589.6 3.3 copy.27
  (91 shorter events, 3.9 us)
Async XLA Ops:
  7.2 44.9 %copy-start = (bf16[768,1536]{1,0:T(8,128)(2,1)S(1)}, bf16[768,1536]{1,0:T(8,128)(2,1)}, u32[]{:S(2)}) copy-start(bf16[768,1536]{1,0:T(8,128)(2,1)} %param.18) | copy-start | bytes 7077892
  12.9 26.1 %all-to-all-start = ((bf16[16,4,8,768]{3,2,1,0:T(8,128)(2,1)}), bf16[16,4,8,768]{3,2,1,0:T(8,128)(2,1)S(1)}, u32[]{:S(2)}, u32[]{:S(2)}) async-start(bf16[16,4,8,768]{3,2,1,0:T(8,128)(2,1)} %bitcast.63), calls=%async_computation | async-start | bytes 1572864 | tf_op jit(solution)/shard_map/all_to_all | solution.py:235
  20.2 31.9 %all-gather.8.cloned.1.call-start = ((), (), s32[]{:S(2)}) async-start(), calls=%async_computation.8 | async-start | bytes 2359296 | tf_op jit(solution)/shard_map/all_gather | solution.py:232
  23.3 19.4 %copy-start.17 = (s32[512]{0:T(512)S(1)}, s32[512]{0:T(512)}, u32[]{:S(2)}) copy-start(s32[512]{0:T(512)} %param.21) | copy-start | bytes 6148
  23.4 19.8 %copy-start.15 = (f32[768]{0:T(1024)S(1)}, f32[768]{0:T(1024)}, u32[]{:S(2)}) copy-start(f32[768]{0:T(1024)} %param.16) | copy-start | bytes 9220
  23.4 19.8 %copy-start.16 = (f32[768]{0:T(1024)S(1)}, f32[768]{0:T(1024)}, u32[]{:S(2)}) copy-start(f32[768]{0:T(1024)} %param.17) | copy-start | bytes 9220
  23.4 58.1 %all-gather.6.cloned.1.call-start = ((), (), s32[]{:S(2)}) async-start(), calls=%async_computation.7 | async-start | bytes 2359296 | tf_op jit(solution)/shard_map/all_gather | solution.py:248
  38.9 0.9 copy-start.13
  41.5 1.2 copy-start.11
  42.7 135.8 %reduce-scatter.12.cloned.1.call-start = ((), (), s32[]{:S(2)}) async-start(), calls=%async_computation.13 | async-start | bytes 2506752 | tf_op jit(solution)/shard_map/reduce_scatter | solution.py:300
  81.4 1.9 copy-start.9
  81.4 2.4 copy-start.18
  81.4 2.4 copy-start.19
  83.9 5.1 copy-start.1
  83.9 5.1 copy-start.2
  109.7 0.9 copy-start.3
  110.6 0.9 copy-start.7
  111.5 0.9 copy-start.5
  115.4 1.1 copy-start.8
  115.4 129.8 %reduce-scatter.10.cloned.1.call-start = ((), (), s32[]{:S(2)}) async-start(), calls=%async_computation.11 | async-start | bytes 2506752 | tf_op jit(solution)/shard_map/reduce_scatter | solution.py:300
  120.9 1.1 copy-start.4
  120.9 190.0 %reduce-scatter.14.cloned.1.call-start = ((), (), s32[]{:S(2)}) async-start(), calls=%async_computation.15 | async-start | bytes 2506752 | tf_op jit(solution)/shard_map/reduce_scatter | solution.py:300
  126.4 211.8 %reduce-scatter.8.cloned.1.call-start = ((), (), s32[]{:S(2)}) async-start(), calls=%async_computation.10 | async-start | bytes 2359296 | tf_op jit(solution)/shard_map/reduce_scatter | solution.py:270
  126.4 3.6 copy-start.6
  126.4 3.6 copy-start.10
  134.8 256.5 %reduce-scatter.6.cloned.1.call-start = ((), (), s32[]{:S(2)}) async-start(), calls=%async_computation.9 | async-start | bytes 2359296 | tf_op jit(solution)/shard_map/reduce_scatter | solution.py:283
  137.4 200.8 %copy-start.12 = (bf16[64,8,768]{2,1,0:T(8,128)(2,1)S(1)}, bf16[64,8,768]{2,1,0:T(8,128)(2,1)}, u32[]{:S(2)}) copy-start(bf16[64,8,768]{2,1,0:T(8,128)(2,1)} %copy-done.11) | copy-start | bytes 2359300
  137.4 274.7 %all-gather.12.cloned.1.call-start = ((), (), s32[]{:S(2)}) async-start(), calls=%async_computation.14 | async-start | bytes 2506752 | tf_op jit(solution)/shard_map/all_gather | solution.py:301
  178.5 277.3 %all-gather.10.cloned.1.call-start = ((), (), s32[]{:S(2)}) async-start(), calls=%async_computation.12 | async-start | bytes 2506752 | tf_op jit(solution)/shard_map/all_gather | solution.py:301
  245.3 254.0 %all-gather.14.cloned.1.call-start = ((), (), s32[]{:S(2)}) async-start(), calls=%async_computation.16 | async-start | bytes 2506752 | tf_op jit(solution)/shard_map/all_gather | solution.py:301
  343.8 50.0 %all-to-all-start.1 = ((bf16[16,4,8,768]{3,2,1,0:T(8,128)(2,1)}), bf16[16,4,8,768]{3,2,1,0:T(8,128)(2,1)S(1)}, u32[]{:S(2)}, u32[]{:S(2)}) async-start(bf16[16,4,8,768]{3,2,1,0:T(8,128)(2,1)} %bitcast.14), calls=%async_computation.3 | async-start | bytes 1572864 | tf_op jit(solution)/shard_map/all_to_all | solution.py:318
  349.4 240.2 %all-reduce.3.cloned.1.call-start = ((), (), s32[]{:S(2)}) async-start(), calls=%async_computation.17 | async-start | bytes 196608 | tf_op jit(solution)/shard_map/psum | solution.py:306
  589.6 3.3 copy-start.14
Sparse Core Ops, SparseCore 0:
  23.5 28.5 all-gather.7
  54.2 27.2 all-gather.5
  115.5 62.9 reduce-scatter.11
  183.2 62.0 reduce-scatter.9
  248.8 61.9 reduce-scatter.13
  313.1 25.0 reduce-scatter.7
  340.4 26.6 reduce-scatter.5
  369.7 42.3 all-gather.11
  414.6 41.0 all-gather.9
  458.1 41.0 all-gather.13
  503.7 85.8 all-reduce.2

commit v2 on v1

--- a/solution.py
+++ b/solution.py
@@ -171,6 +171,158 @@
     return [result[:, :given] for result in results] if channels != given else results
 
 
+def sum_kernel(chunk, per_array, orders, n, *refs):
+    arrays = len(per_array)
+    bits = len(orders[0])
+    ins, small_in = refs[:arrays], refs[arrays]
+    stacked_out, last_out, small_out = refs[arrays + 1 : arrays + 4]
+    red, got, small_buf, small_got, sends, recvs, small_sends, small_recvs = refs[arrays + 4 :]
+    me = lax.axis_index("dp")
+    digit = [(me // (1 << b)) % 2 for b in range(bits)]
+    partner = [me + (1 - 2 * digit[b]) * (1 << b) for b in range(bits)]
+    places = [(a, i * chunk) for a in range(arrays) for i in range(per_array[a])]
+    chunks = range(len(places))
+    lengths = [chunk >> (s + 1) for s in range(bits)]
+    bases = [chunk - 2 * lengths[s] for s in range(bits)]
+
+    def target(c, start, size):
+        a, first = places[c]
+        rows = pl.ds(pl.multiple_of(first + start, 16), size)
+        return stacked_out.at[a, rows] if a < arrays - 1 else last_out.at[rows]
+
+    def held(c, s, start, size):
+        if s == 0:
+            a, first = places[c]
+            return ins[a].at[pl.ds(pl.multiple_of(first + start, 16), size)]
+        return red.at[c, pl.ds(pl.multiple_of(bases[s - 1] + start, 16), size)]
+
+    def halving(c, s):
+        b = orders[c][s]
+        return pltpu.make_async_remote_copy(
+            src_ref=held(c, s, (1 - digit[b]) * lengths[s], lengths[s]),
+            dst_ref=got.at[c, pl.ds(bases[s], lengths[s])],
+            send_sem=sends.at[s, c],
+            recv_sem=recvs.at[s, c],
+            device_id={"dp": partner[b]},
+            device_id_type=pl.DeviceIdType.MESH,
+        )
+
+    def offset(c, s):
+        return sum(digit[orders[c][k]] * lengths[k] for k in range(s + 1))
+
+    def doubling(c, s):
+        b = orders[c][s]
+        place = target(c, offset(c, s), lengths[s])
+        return pltpu.make_async_remote_copy(
+            src_ref=place,
+            dst_ref=place,
+            send_sem=sends.at[bits + s, c],
+            recv_sem=recvs.at[bits + s, c],
+            device_id={"dp": partner[b]},
+            device_id_type=pl.DeviceIdType.MESH,
+        )
+
+    def small_copy(s):
+        return pltpu.make_async_remote_copy(
+            src_ref=small_buf.at[s],
+            dst_ref=small_got.at[s],
+            send_sem=small_sends.at[s],
+            recv_sem=small_recvs.at[s],
+            device_id={"dp": partner[s]},
+            device_id_type=pl.DeviceIdType.MESH,
+        )
+
+    barrier = pltpu.get_barrier_semaphore()
+    for b in range(bits):
+        pl.semaphore_signal(
+            barrier, inc=1, device_id={"dp": partner[b]}, device_id_type=pl.DeviceIdType.MESH
+        )
+    pl.semaphore_wait(barrier, bits)
+
+    small_buf[0] = small_in[...]
+    small_copy(0).start()
+    for c in chunks:
+        halving(c, 0).start()
+    for s in range(bits):
+        for c in chunks:
+            halving(c, s).wait_recv()
+            kept = held(c, s, digit[orders[c][s]] * lengths[s], lengths[s])
+            come = got.at[c, pl.ds(bases[s], lengths[s])]
+            if s < bits - 1:
+                into = red.at[c, pl.ds(bases[s], lengths[s])]
+            else:
+                into = target(c, offset(c, s), lengths[s])
+
+            @pl.loop(0, lengths[s] // 16)
+            def _(i):
+                rows = pl.ds(pl.multiple_of(i * 16, 16), 16)
+                into[rows, :] = (
+                    kept[rows, :].astype(jnp.float32) + come[rows, :].astype(jnp.float32)
+                ).astype(jnp.bfloat16)
+
+            if s < bits - 1:
+                halving(c, s + 1).start()
+            else:
+                doubling(c, s).start()
+        small_copy(s).wait_recv()
+        total = small_buf[s] + small_got[s]
+        if s < bits - 1:
+            small_buf[s + 1] = total
+            small_copy(s + 1).start()
+        else:
+            small_out[...] = total
+    for s in reversed(range(bits)):
+        for c in chunks:
+            doubling(c, s).wait_recv()
+            if s > 0:
+                doubling(c, s - 1).start()
+    for s in range(bits):
+        small_copy(s).wait_send()
+        for c in chunks:
+            halving(c, s).wait_send()
+            doubling(c, s).wait_send()
+
+
+def sum_over_dp(terms, small, n):
+    rows, width = terms[0].shape
+    bits = n.bit_length() - 1
+    chunk = 16 * n
+    per_array = [term.shape[0] // chunk for term in terms]
+    count = sum(per_array)
+    plain = list(range(bits))
+    turned = [0] + plain[2:] + [1]
+    orders = [turned if c % 4 == 0 and c < 8 else plain for c in range(count)]
+    vmem = pl.BlockSpec(memory_space=pltpu.VMEM)
+    return pl.pallas_call(
+        functools.partial(sum_kernel, chunk, per_array, orders, n),
+        out_shape=(
+            jax.ShapeDtypeStruct((len(terms) - 1, rows, width), jnp.bfloat16),
+            jax.ShapeDtypeStruct((rows, width), jnp.bfloat16),
+            jax.ShapeDtypeStruct(small.shape, jnp.float32),
+        ),
+        in_specs=[vmem] * (len(terms) + 1),
+        out_specs=(vmem, vmem, vmem),
+        scratch_shapes=[
+            pltpu.VMEM((count, chunk, width), jnp.bfloat16),
+            pltpu.VMEM((count, chunk, width), jnp.bfloat16),
+            pltpu.VMEM((bits,) + small.shape, jnp.float32),
+            pltpu.VMEM((bits,) + small.shape, jnp.float32),
+            pltpu.SemaphoreType.DMA((2 * bits, count)),
+            pltpu.SemaphoreType.DMA((2 * bits, count)),
+            pltpu.SemaphoreType.DMA((bits,)),
+            pltpu.SemaphoreType.DMA((bits,)),
+        ],
+        compiler_params=pltpu.CompilerParams(
+            collective_id=0, has_side_effects=True, vmem_limit_bytes=44 * 1024 * 1024
+        ),
+        cost_estimate=pl.CostEstimate(
+            flops=count * chunk * width,
+            bytes_accessed=4 * count * chunk * width,
+            transcendentals=0,
+        ),
+    )(*terms, small)
+
+
 def on_device(
     frames,
     norm_gain,
@@ -267,6 +419,9 @@
         jnp.dot(delta_linear, input_weight[0], preferred_element_type=jnp.float32)
         + jnp.dot(delta_gate, input_weight[1], preferred_element_type=jnp.float32)
     ).astype(jnp.bfloat16)
+    back_term, swish, delta_linear, delta_gate = lax.optimization_barrier(
+        (back_term, swish, delta_linear, delta_gate)
+    )
     delta_normed = lax.psum_scatter(back_term, "tensor", scatter_dimension=1, tiled=True).astype(
         jnp.float32
     )
@@ -275,10 +430,7 @@
     unit_local = jnp.sum(back_float * norm_gain, axis=1)
     cross_local = jnp.sum(back_standard * norm_gain, axis=1)
     unit_total, cross_total = lax.psum((unit_local, cross_local), "tensor")
-    norm_sums = lax.psum(
-        jnp.stack([jnp.sum(back_standard, axis=0), jnp.sum(back_float, axis=0)]), ("dp", "tensor")
-    )
-    norm_part = lax.dynamic_slice_in_dim(norm_sums, column_start, part_width, 1)
+    norm_local = jnp.stack([jnp.sum(back_standard, axis=0), jnp.sum(back_float, axis=0)])
 
     mixed_sum = lax.psum_scatter(
         jnp.dot(swish, output_weight, preferred_element_type=jnp.float32).astype(jnp.bfloat16),
@@ -296,14 +448,11 @@
             left, right, (((0,), (0,)), ((), ())), preferred_element_type=jnp.float32
         ).astype(jnp.bfloat16)
 
-    def summed(term):
-        piece = lax.psum_scatter(term, "dp", scatter_dimension=0, tiled=True)
-        return lax.all_gather(piece, "dp", axis=0, tiled=True)
-
-    out_summed = summed(over_rows(swish, delta_whole))
-    linear_summed = summed(over_rows(delta_linear, normed))
-    gate_summed = summed(over_rows(delta_gate, normed))
-    tap_summed = lax.psum(tap_local, "dp")
+    terms = (
+        over_rows(delta_linear, normed),
+        over_rows(delta_gate, normed),
+        over_rows(swish, delta_whole),
+    )
 
     gain_part = lax.dynamic_slice_in_dim(norm_gain, column_start, part_width)
     standard = (local_rows.astype(jnp.float32) - center) * scale_row
@@ -315,6 +464,19 @@
     )
     delta_blocks = delta_rows.astype(jnp.bfloat16).reshape(cap_blocks, BLK, part_width)
     homebound = delta_blocks[landing.reshape(-1)].reshape(replicas, per_peer, BLK, part_width)
+
+    taps = depth_weight.shape[0]
+    small = jnp.concatenate([tap_local, norm_local.reshape(-1, part_width)])
+    homebound, terms, small = lax.optimization_barrier((homebound, terms, small))
+    if part_width % (16 * replicas) == 0 and replicas & (replicas - 1) == 0 and replicas > 2:
+        weight_summed, out_summed, small_summed = sum_over_dp(terms, small, replicas)
+    else:
+        linear_summed, gate_summed, out_summed, small_summed = lax.psum((*terms, small), "dp")
+        weight_summed = jnp.stack([linear_summed, gate_summed])
+    tap_summed = small_summed[:taps]
+    norm_part = lax.psum_scatter(
+        small_summed[taps:].reshape(2, full_width), "tensor", scatter_dimension=1, tiled=True
+    )
     returned = lax.all_to_all(homebound, "dp", split_axis=0, concat_axis=0, tiled=True)
     frame_gradient = returned.reshape(replicas * per_peer, BLK, part_width)[pick_back].reshape(
         load_rows, part_width
@@ -322,7 +484,7 @@
     return (
         block_output,
         frame_gradient,
-        jnp.stack([linear_summed, gate_summed]),
+        weight_summed,
         out_summed,
         tap_summed,
         norm_part[0],

time: 601 us -> 316 us (0.53)
  waiting for transfers between devices: 434 us -> 67.9 us
  Pallas kernels: 20.7 us -> 140 us
  blocking collectives: 45.4 us -> 5.18 us
  local copies, waits for them, and re-layouts: 20.3 us -> 29 us
    reduce_scatter x3 -> x0, waiting for transfers between devices: 173 us -> none  [summed(): piece = lax.psum_scatter(term, 'dp', scatter_dimension=0, tiled=True)]
    pallas_call x0 -> x1, Pallas kernels: none -> 120 us  [sum_over_dp(): pl.pallas_call(functools.partial(sum_kernel, chunk, per_array, orders, n)...]
    all_gather x3 -> x0, waiting for transfers between devices: 99.2 us -> none  [summed(): return lax.all_gather(piece, 'dp', axis=0, tiled=True)]
    psum x1 -> x0, waiting for transfers between devices: 90.3 us -> none  [on_device(): tap_summed = lax.psum(tap_local, 'dp')]
    psum x1 -> x0, blocking collectives: 40.4 us -> none  [on_device(): lax.psum(jnp.stack([jnp.sum(back_standard, axis=0), jnp.sum(back_float, a...]
    reduce_scatter x1, waiting for transfers between devices: 21.4 us -> 3.84 us  [on_device(): lax.psum_scatter(back_term, 'tensor', scatter_dimension=1, tiled=True)]
    unnamed x11 -> x6, waiting for transfers between devices: 0.59 us -> 15 us
    unnamed x42 -> x55, local copies, waits for them, and re-layouts: 9.72 us -> 15.1 us
  transfers between devices with their start and end apart: 13 -> 7, of which waited for: 11 -> 5; matrix products, arithmetic and copies ran while one was open for 8% -> 13% of each run, Pallas kernels for 0% -> 38%
where the time goes in v2:
time: 316 us; the launch traced here: 315 us
  Pallas kernels  140 us (44%)
  waiting for transfers between devices  67.9 us (21%)
  local copies, waits for them, and re-layouts  29 us (9%)
  matrix products  26.2 us (8%)
  other arithmetic  18.8 us (6%)
  between operations  14.2 us (4%)
  starting transfers between devices  13.2 us (4%)
  blocking collectives  5.18 us (2%)
    pallas_call x1, Pallas kernels, sum_over_dp(): pl.pallas_call(functools.partial(sum_kernel, chunk, per_array, orders, n)...  120 us
    all_gather x1, waiting for transfers between devices, on_device(): gathered = lax.all_gather(local_rows, 'tensor', axis=1, tiled=True)  25.4 us
    pallas_call x1, Pallas kernels, conv_both(): pl.pallas_call(functools.partial(conv_kernel, taps, taps // 2, tile), gri...  20.1 us
    unnamed x55, local copies, waits for them, and re-layouts  15.1 us
    unnamed x6, waiting for transfers between devices  15 us
    all_to_all x1, waiting for transfers between devices, on_device(): lax.all_to_all(outbox.reshape(replicas, per_peer, BLK, part_width), 'dp',...  14.8 us
    dot_general x3, matrix products, over_rows(): lax.dot_general(left, right, (((0,), (0,)), ((), ())), preferred_element_...  10.4 us
    all_gather x1, waiting for transfers between devices, on_device(): delta_whole = lax.all_gather(delta_piece, 'tensor', axis=0, tiled=True)  8.9 us
  transfers between devices with their start and end apart: 7, of which 5 were waited for; matrix products, arithmetic and copies ran while one was open for 13% of the time, Pallas kernels for 38%

profile of v2, /device:TPU:0, one launch (start us, length us, event | category | flops | bytes accessed | tf_op | source)
XLA Modules:
  0.0 314.8 jit_solution(1534604842816831051)
XLA Ops:
  7.2 0.9 copy.25
  8.1 0.1 reduce
  8.2 1.3 fusion.17
  9.5 0.7 and_select_fusion.1
  10.4 2.5 gather_fusion
  12.9 7.4 %all-to-all-start = ((bf16[16,4,8,768]{3,2,1,0:T(8,128)(2,1)}), bf16[16,4,8,768]{3,2,1,0:T(8,128)(2,1)S(1)}, u32[]{:S(2)}, u32[]{:S(2)}) async-start(bf16[16,4,8,768]{3,2,1,0:T(8,128)(2,1)} %bitcast.61), calls=%async_computation | async-start | bytes 1572864 | tf_op jit(solution)/shard_map/all_to_all | solution.py:387
  20.3 0.7 iota_compare_fusion.1
  21.2 2.1 broadcast_select_fusion
  23.4 0.7 fusion.19
  24.1 14.8 %all-to-all-done = bf16[16,4,8,768]{3,2,1,0:T(8,128)(2,1)S(1)} async-done(((bf16[16,4,8,768]{3,2,1,0:T(8,128)(2,1)}), bf16[16,4,8,768]{3,2,1,0:T(8,128)(2,1)S(1)}, u32[]{:S(2)}, u32[]{:S(2)}) %all-to-all-start) | async-done | bytes 786464 | tf_op jit(solution)/shard_map/all_to_all | solution.py:387
  38.9 0.9 copy-done.18
  39.8 1.7 gather_fusion.1
  41.6 1.1 bitcast_select_fusion
  42.9 0.1 convert_element_type.80.active_ref
  43.0 0.1 copy.26.seg_ref
  43.2 8.9 %all-gather.5.cloned.1.call-done = bf16[512,1536]{1,0:T(8,128)(2,1)} async-done(((bf16[256,1536]{1,0:T(8,128)(2,1)}), bf16[512,1536]{1,0:T(8,128)(2,1)}) %all-gather.5.cloned.1.call-update) | async-done | bytes 1572880 | tf_op jit(solution)/shard_map/all_gather | solution.py:384
  52.1 4.0 %fusion.26.delta_ref = f32[512,768]{1,0:T(8,128)} fusion(bf16[512,1536]{1,0:T(8,128)(2,1)} %all-gather.5.cloned.1.call-done, bf16[768,1536]{1,0:T(8,128)(2,1)S(1)} %copy-done), kind=kOutput, calls=%fused_computation.91 | convolution fusion | flops 1207959552 | bytes 5505024 | tf_op jit(solution)/shard_map/dot_general | solution.py:402
  56.0 25.4 %all-gather.3.cloned.1.call-done = bf16[512,1536]{1,0:T(8,128)(2,1)} async-done(((bf16[512,768]{1,0:T(8,128)(2,1)}), bf16[512,1536]{1,0:T(8,128)(2,1)}) %all-gather.3.cloned.1.call-update) | async-done | bytes 1572880 | tf_op jit(solution)/shard_map/all_gather | solution.py:400
  81.4 1.8 convert_reduce_fusion.1
  83.3 0.5 fusion.5
  83.9 5.3 %convolution_bitcast_fusion.linear_ref.gate_ref = f32[2,512,768]{2,1,0:T(8,128)S(1)} fusion(bf16[2,768,1536]{2,1,0:T(8,128)(2,1)} %param.14, bf16[512,1536]{1,0:T(8,128)(2,1)S(1)} %copy-done.14, f32[1536]{0:T(1024)S(1)} %copy-done.23, f32[1536]{0:T(1024)S(1)} %copy-done.19, f32[512]{0:T(512)S(1)} %add_rsqrt_fusion, f32[512]{0:T(512)S(1)} %broadcast_multiply_fusion.2), kind=kOutput, calls=%fused_computation.29 | convolution fusion | flops 2420637696 | bytes 9453568 | tf_op jit(solution)/shard_map/td,kcd->ktc/dot_general | solution.py:412
  89.3 20.1 %shard_map.162 = (bf16[512,768]{1,0:T(8,128)(2,1)S(1)}, bf16[512,768]{1,0:T(8,128)(2,1)S(1)}, bf16[512,768]{1,0:T(8,128)(2,1)S(1)}, f32[32,768]{1,0:T(8,128)S(1)}) custom-call(f32[2,512,768]{2,1,0:T(8,128)S(1)} %convolution_bitcast_fusion.linear_ref.gate_ref, f32[2,512,768]{2,1,0:T(8,128)S(1)} %convolution_bitcast_fusion.linear_ref.gate_ref, ...), custom_call_target="tpu_custom_call" | custom-call | flops 125829120 | bytes 7077888 | tf_op jit(solution)/shard_map/pallas_call | solution.py:129
  109.4 1.4 fusion.10
  110.9 2.6 fusion.7
  113.7 0.7 subtract_clamp_fusion
  114.5 2.5 convolution_convert_fusion.3
  117.1 3.2 %fusion.8 = (f32[1536]{0:T(1024)S(1)}, f32[512]{0:T(512)S(1)}, f32[512]{0:T(512)S(1)}, f32[1536]{0:T(1024)S(1)}) fusion(bf16[512,1536]{1,0:T(8,128)(2,1)} %all-gather.3.cloned.1.call-done, bf16[512,1536]{1,0:T(8,128)(2,1)} %fusion.7, f32[512]{0:T(512)S(1)} %add_rsqrt_fusion, f32[512]{0:T(512)S(1)} %broadcast_multiply_fusion.2, f32[1536]{0:T(1024)S(1)} %copy-done.19), kind=kLoop, calls=%fused_computation.23 | loop fusion | flops 8646656 | bytes 3172352 | tf_op jit(solution)/shard_map/reduce_sum | solution.py:433
  120.4 5.2 %all-reduce = (f32[512]{0:T(512)S(1)}, f32[512]{0:T(512)S(1)}) all-reduce(f32[512]{0:T(512)S(1)} %get-tuple-element.40, f32[512]{0:T(512)S(1)} %get-tuple-element.41), channel_id=1, replica_groups=mesh['dp'=16,'tensor'=2] {'tensor'}, use_global_device_ids=true, to_apply=%region_10.11 | all-reduce | flops 1024 | bytes 8192 | tf_op jit(solution)/shard_map/psum | solution.py:432
  125.6 4.4 %convolution_convert_fusion.refs_2_ = bf16[768,1536]{1,0:T(8,128)(2,1)} fusion(bf16[512,768]{1,0:T(8,128)(2,1)S(1)} %copy-done.13, bf16[512,1536]{1,0:T(8,128)(2,1)} %all-gather.5.cloned.1.call-done), kind=kOutput, calls=%fused_computation.12 | convolution fusion | flops 1209139200 | bytes 4718592 | tf_op jit(solution)/shard_map/dot_general | solution.py:447
  130.0 3.0 convolution_convert_fusion.1.refs_1_
  133.0 3.0 convolution_convert_fusion.2.refs_0_
  136.0 3.8 %reduce-scatter.8.cloned.1.call-done = bf16[512,768]{1,0:T(8,128)(2,1)} async-done(((bf16[512,1536]{1,0:T(8,128)(2,1)}), bf16[512,768]{1,0:T(8,128)(2,1)}) %reduce-scatter.8.cloned.1.call-update) | async-done | bytes 786448 | tf_op jit(solution)/shard_map/reduce_scatter | solution.py:425
  139.9 3.0 fusion.15
  142.8 2.7 gather_fusion.2
  145.5 5.7 %all-to-all-start.1 = ((bf16[16,4,8,768]{3,2,1,0:T(8,128)(2,1)}), bf16[16,4,8,768]{3,2,1,0:T(8,128)(2,1)}, u32[]{:S(2)}, u32[]{:S(2)}) async-start(bf16[16,4,8,768]{3,2,1,0:T(8,128)(2,1)} %bitcast.14), calls=%async_computation.3 | async-start | bytes 1572864 | tf_op jit(solution)/shard_map/all_to_all | solution.py:480
  151.5 1.7 copy-done.3
  153.1 1.7 copy-done.4
  154.8 1.7 copy-done.5
  156.5 120.1 %shard_map.163 = (bf16[2,768,1536]{2,1,0:T(8,128)(2,1)}, bf16[768,1536]{1,0:T(8,128)(2,1)S(1)}, f32[36,768]{1,0:T(8,128)S(1)}) custom-call(bf16[768,1536]{1,0:T(8,128)(2,1)S(1)} %copy-done.5, bf16[768,1536]{1,0:T(8,128)(2,1)S(1)} %copy-done.4, bf16[768,1536]{1,0:T(8,128)(2,1)S(1)} %copy-done.3, f32[36,768]{1,0:T(8,128)S(1)} %pad_maximum_fusion.refs_3_), custom_call_target="tpu_custom_call" | custom-call | flops 3538944 | bytes 14155776 | tf_op jit(solution)/shard_map/pallas_call | solution.py:296
  276.6 1.4 copy-done.1
  278.1 1.2 copy.28
  279.3 2.5 select_convert_fusion
  281.8 0.6 slice.20
  282.5 14.9 %reduce-scatter.10.cloned.1.call-done = f32[768,2]{1,0:T(8,128)} async-done(((f32[1536,2]{1,0:T(8,128)}), f32[768,2]{1,0:T(8,128)}) %reduce-scatter.10.cloned.1.call-update) | async-done | bytes 6160
  297.3 2.1 slice_reduce_fusion
  299.4 2.5 gather_fusion.3
  301.9 5.0 %copy.36 = bf16[2,768,1536]{2,1,0:T(8,128)(2,1)} copy(bf16[2,768,1536]{2,1,0:T(8,128)(2,1)} %get-tuple-element.63) | data formatting | bytes 9437184
  306.9 1.4 copy.37
  (92 shorter events, 1.5 us)
Async XLA Ops:
  7.2 44.9 %copy-start = (bf16[768,1536]{1,0:T(8,128)(2,1)S(1)}, bf16[768,1536]{1,0:T(8,128)(2,1)}, u32[]{:S(2)}) copy-start(bf16[768,1536]{1,0:T(8,128)(2,1)} %param.18) | copy-start | bytes 7077892
  12.9 26.1 %all-to-all-start = ((bf16[16,4,8,768]{3,2,1,0:T(8,128)(2,1)}), bf16[16,4,8,768]{3,2,1,0:T(8,128)(2,1)S(1)}, u32[]{:S(2)}, u32[]{:S(2)}) async-start(bf16[16,4,8,768]{3,2,1,0:T(8,128)(2,1)} %bitcast.61), calls=%async_computation | async-start | bytes 1572864 | tf_op jit(solution)/shard_map/all_to_all | solution.py:387
  20.2 31.9 %all-gather.5.cloned.1.call-start = ((), (), s32[]{:S(2)}) async-start(), calls=%async_computation.6 | async-start | bytes 2359296 | tf_op jit(solution)/shard_map/all_gather | solution.py:384
  23.3 19.4 %copy-start.20 = (f32[768]{0:T(1024)S(1)}, f32[768]{0:T(1024)}, u32[]{:S(2)}) copy-start(f32[768]{0:T(1024)} %param.16) | copy-start | bytes 9220
  23.3 19.5 %copy-start.21 = (f32[768]{0:T(1024)S(1)}, f32[768]{0:T(1024)}, u32[]{:S(2)}) copy-start(f32[768]{0:T(1024)} %param.17) | copy-start | bytes 9220
  23.3 19.7 %copy-start.22 = (s32[512]{0:T(512)S(1)}, s32[512]{0:T(512)}, u32[]{:S(2)}) copy-start(s32[512]{0:T(512)} %param.21) | copy-start | bytes 6148
  23.4 58.1 %all-gather.3.cloned.1.call-start = ((), (), s32[]{:S(2)}) async-start(), calls=%async_computation.5 | async-start | bytes 2359296 | tf_op jit(solution)/shard_map/all_gather | solution.py:400
  38.9 0.9 copy-start.18
  41.5 1.2 copy-start.16
  42.7 97.1 %reduce-scatter.8.cloned.1.call-start = ((), (), s32[]{:S(2)}) async-start(), calls=%async_computation.8 | async-start | bytes 2359296 | tf_op jit(solution)/shard_map/reduce_scatter | solution.py:425
  81.4 1.9 copy-start.14
  81.4 2.4 copy-start.19
  81.4 2.4 copy-start.23
  83.3 26.1 %slice-start = ((s8[4718592]{0:T(1024)(128)(4,1)}), s8[4194304]{0:T(1024)(128)(4,1)S(1)}, s32[]{:S(2)}) async-start(s8[4718592]{0:T(1024)(128)(4,1)} %bitcast.68), calls=%async_computation.10 | async-start | bytes 8388608
  83.9 5.4 %copy-start.6 = (f32[512,768]{1,0:T(8,128)S(1)}, f32[512,768]{1,0:T(8,128)}, u32[]{:S(2)}) copy-start(f32[512,768]{1,0:T(8,128)} %fusion.26.delta_ref) | copy-start | bytes 4718596
  83.9 5.4 %copy-start.7 = (f32[32,768]{1,0:T(8,128)S(1)}, f32[32,768]{1,0:T(8,128)}, u32[]{:S(2)}) copy-start(f32[32,768]{1,0:T(8,128)} %weight_ref.1) | copy-start | bytes 294916
  83.9 25.5 %slice-start.1 = ((s8[4718592]{0:T(1024)(128)(4,1)}), s8[524288]{0:T(1024)(128)(4,1)S(1)}, s32[]{:S(2)}) async-start(s8[4718592]{0:T(1024)(128)(4,1)} %bitcast.68), calls=%async_computation.11 | async-start | bytes 1048576
  109.4 1.5 copy-start.8
  109.4 1.5 copy-start.12
  109.4 1.4 copy-start.10
  110.9 3.6 %copy-start.13 = (bf16[512,768]{1,0:T(8,128)(2,1)S(1)}, bf16[512,768]{1,0:T(8,128)(2,1)}, u32[]{:S(2)}) copy-start(bf16[512,768]{1,0:T(8,128)(2,1)} %copy-done.12) | copy-start | bytes 2359300
  113.5 165.8 %reduce-scatter.6.cloned.1.call-start = ((), (), s32[]{:S(2)}) async-start(), calls=%async_computation.7 | async-start | bytes 2359296 | tf_op jit(solution)/shard_map/reduce_scatter | solution.py:435
  125.6 4.4 %copy-start.11 = (bf16[512,768]{1,0:T(8,128)(2,1)S(1)}, bf16[512,768]{1,0:T(8,128)(2,1)}, u32[]{:S(2)}) copy-start(bf16[512,768]{1,0:T(8,128)(2,1)} %copy-done.10) | copy-start | bytes 2359300
  125.6 4.4 %copy-start.15 = (bf16[512,1536]{1,0:T(8,128)(2,1)S(1)}, bf16[512,1536]{1,0:T(8,128)(2,1)}, u32[]{:S(2)}) copy-start(bf16[512,1536]{1,0:T(8,128)(2,1)} %all-gather.3.cloned.1.call-done) | copy-start | bytes 4718596
  130.0 3.0 copy-start.9
  133.0 6.8 %copy-start.17 = (bf16[64,8,768]{2,1,0:T(8,128)(2,1)S(1)}, bf16[64,8,768]{2,1,0:T(8,128)(2,1)}, u32[]{:S(2)}) copy-start(bf16[64,8,768]{2,1,0:T(8,128)(2,1)} %copy-done.16) | copy-start | bytes 2359300
  145.5 153.9 %all-to-all-start.1 = ((bf16[16,4,8,768]{3,2,1,0:T(8,128)(2,1)}), bf16[16,4,8,768]{3,2,1,0:T(8,128)(2,1)}, u32[]{:S(2)}, u32[]{:S(2)}) async-start(bf16[16,4,8,768]{3,2,1,0:T(8,128)(2,1)} %bitcast.14), calls=%async_computation.3 | async-start | bytes 1572864 | tf_op jit(solution)/shard_map/all_to_all | solution.py:480
  151.2 146.2 %reduce-scatter.10.cloned.1.call-start = ((), (), s32[]{:S(2)}) async-start(), calls=%async_computation.9 | async-start | bytes 1179648
  151.4 1.7 copy-start.3
  153.1 1.7 copy-start.4
  154.8 1.7 copy-start.5
  276.6 1.4 copy-start.1
  301.9 5.0 %copy-start.2 = (bf16[768,1536]{1,0:T(8,128)(2,1)S(1)}, bf16[768,1536]{1,0:T(8,128)(2,1)}, u32[]{:S(2)}) copy-start(bf16[768,1536]{1,0:T(8,128)(2,1)} %copy-done.1) | copy-start | bytes 7077892
Sparse Core Ops, SparseCore 0:
  23.5 28.5 all-gather.4
  54.2 27.2 all-gather.2
  113.6 26.1 reduce-scatter.7
  142.0 26.0 reduce-scatter.5
  279.4 17.8 reduce-scatter.9

commit v3 on v2

--- a/solution.py
+++ b/solution.py
@@ -171,12 +171,15 @@
     return [result[:, :given] for result in results] if channels != given else results
 
 
-def sum_kernel(chunk, per_array, orders, n, *refs):
+def sum_kernel(chunk, per_array, orders, with_small, *refs):
     arrays = len(per_array)
     bits = len(orders[0])
-    ins, small_in = refs[:arrays], refs[arrays]
-    stacked_out, last_out, small_out = refs[arrays + 1 : arrays + 4]
-    red, got, small_buf, small_got, sends, recvs, small_sends, small_recvs = refs[arrays + 4 :]
+    ins, refs = refs[:arrays], refs[arrays:]
+    if with_small:
+        small_in, stacked_out, small_out, red, got, sends, recvs = refs[:7]
+        small_buf, small_got, small_sends, small_recvs = refs[7:]
+    else:
+        stacked_out, red, got, sends, recvs = refs
     me = lax.axis_index("dp")
     digit = [(me // (1 << b)) % 2 for b in range(bits)]
     partner = [me + (1 - 2 * digit[b]) * (1 << b) for b in range(bits)]
@@ -188,7 +191,7 @@
     def target(c, start, size):
         a, first = places[c]
         rows = pl.ds(pl.multiple_of(first + start, 16), size)
-        return stacked_out.at[a, rows] if a < arrays - 1 else last_out.at[rows]
+        return stacked_out.at[a, rows]
 
     def held(c, s, start, size):
         if s == 0:
@@ -239,8 +242,9 @@
         )
     pl.semaphore_wait(barrier, bits)
 
-    small_buf[0] = small_in[...]
-    small_copy(0).start()
+    if with_small:
+        small_buf[0] = small_in[...]
+        small_copy(0).start()
     for c in chunks:
         halving(c, 0).start()
     for s in range(bits):
@@ -264,63 +268,64 @@
                 halving(c, s + 1).start()
             else:
                 doubling(c, s).start()
-        small_copy(s).wait_recv()
-        total = small_buf[s] + small_got[s]
-        if s < bits - 1:
-            small_buf[s + 1] = total
-            small_copy(s + 1).start()
-        else:
-            small_out[...] = total
+        if with_small:
+            small_copy(s).wait_recv()
+            total = small_buf[s] + small_got[s]
+            if s < bits - 1:
+                small_buf[s + 1] = total
+                small_copy(s + 1).start()
+            else:
+                small_out[...] = total
     for s in reversed(range(bits)):
         for c in chunks:
             doubling(c, s).wait_recv()
             if s > 0:
                 doubling(c, s - 1).start()
     for s in range(bits):
-        small_copy(s).wait_send()
+        if with_small:
+            small_copy(s).wait_send()
         for c in chunks:
             halving(c, s).wait_send()
             doubling(c, s).wait_send()
 
 
-def sum_over_dp(terms, small, n):
+def sum_over_dp(terms, n, collective_id, small=None):
     rows, width = terms[0].shape
     bits = n.bit_length() - 1
     chunk = 16 * n
-    per_array = [term.shape[0] // chunk for term in terms]
+    per_array = [rows // chunk] * len(terms)
     count = sum(per_array)
     plain = list(range(bits))
     turned = [0] + plain[2:] + [1]
-    orders = [turned if c % 4 == 0 and c < 8 else plain for c in range(count)]
+    orders = [turned if c % 4 == 0 and c + 2 < count else plain for c in range(count)]
     vmem = pl.BlockSpec(memory_space=pltpu.VMEM)
+    with_small = small is not None
+    extra = (small,) if with_small else ()
+    small_shapes = [pltpu.VMEM((bits,) + e.shape, jnp.float32) for e in extra * 2]
+    small_semaphores = [pltpu.SemaphoreType.DMA((bits,)) for e in extra * 2]
     return pl.pallas_call(
-        functools.partial(sum_kernel, chunk, per_array, orders, n),
-        out_shape=(
-            jax.ShapeDtypeStruct((len(terms) - 1, rows, width), jnp.bfloat16),
-            jax.ShapeDtypeStruct((rows, width), jnp.bfloat16),
-            jax.ShapeDtypeStruct(small.shape, jnp.float32),
-        ),
-        in_specs=[vmem] * (len(terms) + 1),
-        out_specs=(vmem, vmem, vmem),
+        functools.partial(sum_kernel, chunk, per_array, orders, with_small),
+        out_shape=[jax.ShapeDtypeStruct((len(terms), rows, width), jnp.bfloat16)]
+        + [jax.ShapeDtypeStruct(e.shape, jnp.float32) for e in extra],
+        in_specs=[vmem] * (len(terms) + len(extra)),
+        out_specs=[vmem] * (1 + len(extra)),
         scratch_shapes=[
             pltpu.VMEM((count, chunk, width), jnp.bfloat16),
             pltpu.VMEM((count, chunk, width), jnp.bfloat16),
-            pltpu.VMEM((bits,) + small.shape, jnp.float32),
-            pltpu.VMEM((bits,) + small.shape, jnp.float32),
             pltpu.SemaphoreType.DMA((2 * bits, count)),
             pltpu.SemaphoreType.DMA((2 * bits, count)),
-            pltpu.SemaphoreType.DMA((bits,)),
-            pltpu.SemaphoreType.DMA((bits,)),
-        ],
+        ]
+        + small_shapes
+        + small_semaphores,
         compiler_params=pltpu.CompilerParams(
-            collective_id=0, has_side_effects=True, vmem_limit_bytes=44 * 1024 * 1024
+            collective_id=collective_id, has_side_effects=True, vmem_limit_bytes=36 * 1024 * 1024
         ),
         cost_estimate=pl.CostEstimate(
             flops=count * chunk * width,
             bytes_accessed=4 * count * chunk * width,
             transcendentals=0,
         ),
-    )(*terms, small)
+    )(*terms, *extra)
 
 
 def on_device(
@@ -380,8 +385,8 @@
     active_rows = jnp.repeat(active, BLK)
     active_mine = lax.dynamic_slice_in_dim(active_rows, row_start, rows_part)[:, None]
 
-    delta_piece = jnp.where(active_mine, upstream, jnp.zeros_like(upstream))
-    delta_whole = lax.all_gather(delta_piece, "tensor", axis=0, tiled=True)
+    upstream_whole = lax.all_gather(upstream, "tensor", axis=0, tiled=True)
+    delta_whole = jnp.where(active_rows[:, None], upstream_whole, jnp.zeros_like(upstream_whole))
 
     outbox = frames.reshape(load_blocks, BLK, part_width)[send_block.reshape(-1)]
     arrived = lax.all_to_all(
@@ -425,34 +430,40 @@
     delta_normed = lax.psum_scatter(back_term, "tensor", scatter_dimension=1, tiled=True).astype(
         jnp.float32
     )
-    back_float = back_term.astype(jnp.float32)
-    back_standard = back_float * standard_full
-    unit_local = jnp.sum(back_float * norm_gain, axis=1)
-    cross_local = jnp.sum(back_standard * norm_gain, axis=1)
+    mixed_term = jnp.dot(swish, output_weight, preferred_element_type=jnp.float32).astype(
+        jnp.bfloat16
+    )
+    mixed_sum = lax.psum_scatter(
+        mixed_term, "tensor", scatter_dimension=0, tiled=True
+    ).astype(jnp.float32)
+    back_float = back_term.astype(jnp.float32) * norm_gain
+    unit_local = jnp.sum(back_float, axis=1)
+    cross_local = jnp.sum(back_float * standard_full, axis=1)
     unit_total, cross_total = lax.psum((unit_local, cross_local), "tensor")
-    norm_local = jnp.stack([jnp.sum(back_standard, axis=0), jnp.sum(back_float, axis=0)])
-
-    mixed_sum = lax.psum_scatter(
-        jnp.dot(swish, output_weight, preferred_element_type=jnp.float32).astype(jnp.bfloat16),
-        "tensor",
-        scatter_dimension=0,
-        tiled=True,
-    ).astype(jnp.float32)
+
+    def over_rows(left, right):
+        return lax.dot_general(
+            left, right, (((0,), (0,)), ((), ())), preferred_element_type=jnp.float32
+        ).astype(jnp.bfloat16)
+
+    by_kernel = (
+        part_width % (16 * replicas) == 0 and replicas & (replicas - 1) == 0 and replicas > 2
+    )
+    terms = (over_rows(delta_linear, normed), over_rows(delta_gate, normed))
+    if by_kernel:
+        terms, mixed_term, swish = lax.optimization_barrier((terms, mixed_term, swish))
+        weight_summed = sum_over_dp(terms, replicas, 1)[0]
+        delta_normed, swish, weight_summed = lax.optimization_barrier(
+            (delta_normed, swish, weight_summed)
+        )
+    else:
+        weight_summed = lax.psum(jnp.stack(terms), "dp")
+    out_term = over_rows(swish, delta_whole)
+
     residual_part = lax.dynamic_slice_in_dim(gathered, row_start, rows_part, 0)
     block_output = jnp.where(
         active_mine, residual_part.astype(jnp.float32) + mixed_sum, 0.0
     ).astype(jnp.bfloat16)
-
-    def over_rows(left, right):
-        return lax.dot_general(
-            left, right, (((0,), (0,)), ((), ())), preferred_element_type=jnp.float32
-        ).astype(jnp.bfloat16)
-
-    terms = (
-        over_rows(delta_linear, normed),
-        over_rows(delta_gate, normed),
-        over_rows(swish, delta_whole),
-    )
 
     gain_part = lax.dynamic_slice_in_dim(norm_gain, column_start, part_width)
     standard = (local_rows.astype(jnp.float32) - center) * scale_row
@@ -466,17 +477,14 @@
     homebound = delta_blocks[landing.reshape(-1)].reshape(replicas, per_peer, BLK, part_width)
 
     taps = depth_weight.shape[0]
-    small = jnp.concatenate([tap_local, norm_local.reshape(-1, part_width)])
-    homebound, terms, small = lax.optimization_barrier((homebound, terms, small))
-    if part_width % (16 * replicas) == 0 and replicas & (replicas - 1) == 0 and replicas > 2:
-        weight_summed, out_summed, small_summed = sum_over_dp(terms, small, replicas)
+    norm_local = jnp.stack([jnp.sum(delta_normed * standard, axis=0), jnp.sum(delta_normed, axis=0)])
+    small = jnp.concatenate([tap_local, norm_local])
+    homebound, out_term, small = lax.optimization_barrier((homebound, out_term, small))
+    if by_kernel:
+        out_stack, small_summed = sum_over_dp((out_term,), replicas, 2, small)
+        out_summed = out_stack[0]
     else:
-        linear_summed, gate_summed, out_summed, small_summed = lax.psum((*terms, small), "dp")
-        weight_summed = jnp.stack([linear_summed, gate_summed])
-    tap_summed = small_summed[:taps]
-    norm_part = lax.psum_scatter(
-        small_summed[taps:].reshape(2, full_width), "tensor", scatter_dimension=1, tiled=True
-    )
+        out_summed, small_summed = lax.psum((out_term, small), "dp")
     returned = lax.all_to_all(homebound, "dp", split_axis=0, concat_axis=0, tiled=True)
     frame_gradient = returned.reshape(replicas * per_peer, BLK, part_width)[pick_back].reshape(
         load_rows, part_width
@@ -486,9 +494,9 @@
         frame_gradient,
         weight_summed,
         out_summed,
-        tap_summed,
-        norm_part[0],
-        norm_part[1],
+        small_summed[:taps],
+        small_summed[taps],
+        small_summed[taps + 1],
     )
 
 

time: 316 us -> 305 us (0.965)
  Pallas kernels: 140 us -> 159 us
  waiting for transfers between devices: 67.9 us -> 49.2 us
  local copies, waits for them, and re-layouts: 29 us -> 25.4 us
    pallas_call x1 -> x2, Pallas kernels: 120 us -> 139 us  [sum_over_dp(): pl.pallas_call(functools.partial(sum_kernel, chunk, per_array, orders, wi...]
    unnamed x6 -> x4, waiting for transfers between devices: 15 us -> 0.73 us
    reduce_scatter x1, waiting for transfers between devices: 3.84 us -> 0.01 us  [on_device(): lax.psum_scatter(back_term, 'tensor', scatter_dimension=1, tiled=True)]
    unnamed x55 -> x56, local copies, waits for them, and re-layouts: 15.1 us -> 14.2 us
  transfers between devices with their start and end apart: 7 -> 6, of which waited for: 5 -> 3; matrix products, arithmetic and copies ran while one was open for 13% -> 11% of each run, Pallas kernels for 38% -> 46%
where the time goes in v3:
time: 305 us; the launch traced here: 304 us
  Pallas kernels  159 us (52%)
  waiting for transfers between devices  49.2 us (16%)
  local copies, waits for them, and re-layouts  25.4 us (8%)
  matrix products  23.5 us (8%)
  other arithmetic  16.2 us (5%)
  between operations  14.3 us (5%)
  starting transfers between devices  11.9 us (4%)
  blocking collectives  4.97 us (2%)
    pallas_call x2, Pallas kernels, sum_over_dp(): pl.pallas_call(functools.partial(sum_kernel, chunk, per_array, orders, wi...  139 us
    all_gather x1, waiting for transfers between devices, on_device(): gathered = lax.all_gather(local_rows, 'tensor', axis=1, tiled=True)  24.1 us
    pallas_call x1, Pallas kernels, conv_both(): pl.pallas_call(functools.partial(conv_kernel, taps, taps // 2, tile), gri...  20.1 us
    all_to_all x1, waiting for transfers between devices, on_device(): lax.all_to_all(outbox.reshape(replicas, per_peer, BLK, part_width), 'dp',...  16.4 us
    unnamed x56, local copies, waits for them, and re-layouts  14.2 us
    dot_general x3, matrix products, over_rows(): lax.dot_general(left, right, (((0,), (0,)), ((), ())), preferred_element_...  9.16 us
    all_gather x1, waiting for transfers between devices, on_device(): upstream_whole = lax.all_gather(upstream, 'tensor', axis=0, tiled=True)  8.05 us
    all_to_all x1, starting transfers between devices, on_device(): lax.all_to_all(outbox.reshape(replicas, per_peer, BLK, part_width), 'dp',...  7.36 us
  transfers between devices with their start and end apart: 6, of which 3 were waited for; matrix products, arithmetic and copies ran while one was open for 11% of the time, Pallas kernels for 46%

profile of v3, /device:TPU:0, one launch (start us, length us, event | category | flops | bytes accessed | tf_op | source)
XLA Modules:
  0.0 304.3 jit_solution(9173726611000454330)
XLA Ops:
  7.2 0.9 copy.22
  8.2 1.3 fusion.18
  9.5 0.7 and_select_fusion.1
  10.4 2.5 gather_fusion
  12.9 7.4 %all-to-all-start = ((bf16[16,4,8,768]{3,2,1,0:T(8,128)(2,1)}), bf16[16,4,8,768]{3,2,1,0:T(8,128)(2,1)S(1)}, u32[]{:S(2)}, u32[]{:S(2)}) async-start(bf16[16,4,8,768]{3,2,1,0:T(8,128)(2,1)} %bitcast.62), calls=%async_computation | async-start | bytes 1572864 | tf_op jit(solution)/shard_map/all_to_all | solution.py:392
  20.3 0.7 all-gather.5.cloned.1.call-update
  21.0 0.7 iota_compare_fusion.1
  21.9 0.7 fusion.20
  22.6 16.4 %all-to-all-done = bf16[16,4,8,768]{3,2,1,0:T(8,128)(2,1)S(1)} async-done(((bf16[16,4,8,768]{3,2,1,0:T(8,128)(2,1)}), bf16[16,4,8,768]{3,2,1,0:T(8,128)(2,1)S(1)}, u32[]{:S(2)}, u32[]{:S(2)}) %all-to-all-start) | async-done | bytes 786464 | tf_op jit(solution)/shard_map/all_to_all | solution.py:392
  38.9 0.9 copy-done.19
  39.8 1.7 gather_fusion.1
  41.6 1.1 bitcast_select_fusion
  43.0 0.1 copy.23.seg_ref
  43.2 8.0 %all-gather.5.cloned.1.call-done = bf16[512,1536]{1,0:T(8,128)(2,1)} async-done(((bf16[256,1536]{1,0:T(8,128)(2,1)}), bf16[512,1536]{1,0:T(8,128)(2,1)}) %all-gather.5.cloned.1.call-update) | async-done | bytes 1572880 | tf_op jit(solution)/shard_map/all_gather | solution.py:388
  51.2 1.6 broadcast_select_fusion
  52.8 1.1 copy-done.17
  54.0 2.6 fusion.27.delta_ref
  56.5 24.1 %all-gather.3.cloned.1.call-done = bf16[512,1536]{1,0:T(8,128)(2,1)} async-done(((bf16[512,768]{1,0:T(8,128)(2,1)}), bf16[512,1536]{1,0:T(8,128)(2,1)}) %all-gather.3.cloned.1.call-update) | async-done | bytes 1572880 | tf_op jit(solution)/shard_map/all_gather | solution.py:405
  80.6 1.8 convert_reduce_fusion
  82.5 0.5 fusion.7
  83.1 5.3 %convolution_bitcast_fusion.linear_ref.gate_ref = f32[2,512,768]{2,1,0:T(8,128)S(1)} fusion(bf16[2,768,1536]{2,1,0:T(8,128)(2,1)} %param.14, bf16[512,1536]{1,0:T(8,128)(2,1)S(1)} %copy-done.12, f32[1536]{0:T(1024)S(1)} %copy-done.24, f32[1536]{0:T(1024)S(1)} %copy-done.20, f32[512]{0:T(512)S(1)} %add_rsqrt_fusion, f32[512]{0:T(512)S(1)} %broadcast_multiply_fusion.2), kind=kOutput, calls=%fused_computation.27 | convolution fusion | flops 2420637696 | bytes 9453568 | tf_op jit(solution)/shard_map/td,kcd->ktc/dot_general | solution.py:417
  88.4 20.1 %shard_map.162 = (bf16[512,768]{1,0:T(8,128)(2,1)S(1)}, bf16[512,768]{1,0:T(8,128)(2,1)S(1)}, bf16[512,768]{1,0:T(8,128)(2,1)S(1)}, f32[32,768]{1,0:T(8,128)S(1)}) custom-call(f32[2,512,768]{2,1,0:T(8,128)S(1)} %convolution_bitcast_fusion.linear_ref.gate_ref, f32[2,512,768]{2,1,0:T(8,128)S(1)} %convolution_bitcast_fusion.linear_ref.gate_ref, ...), custom_call_target="tpu_custom_call" | custom-call | flops 125829120 | bytes 7077888 | tf_op jit(solution)/shard_map/pallas_call | solution.py:129
  108.6 1.4 fusion.11
  110.0 2.5 fusion.9
  112.6 0.2 reduce-scatter.3.cloned.1.call-start
  112.9 0.7 subtract_clamp_fusion
  113.8 2.5 convolution_convert_fusion.3
  116.3 3.4 %convolution_convert_fusion.2.refs_0_ = bf16[768,1536]{1,0:T(8,128)(2,1)S(1)} fusion(bf16[512,768]{1,0:T(8,128)(2,1)} %copy-done.11, bf16[512,1536]{1,0:T(8,128)(2,1)} %all-gather.3.cloned.1.call-done, f32[1536]{0:T(1024)S(1)} %copy-done.24, f32[1536]{0:T(1024)S(1)} %copy-done.20, f32[512]{0:T(512)S(1)} %add_rsqrt_fusion, f32[512]{0:T(512)S(1)} %broadcast_multiply_fusion.2), kind=kOutput, calls=%fused_computation.12 | convolution fusion | flops 1213857792 | bytes 4734976 | tf_op jit(solution)/shard_map/dot_general | solution.py:445
  119.7 1.6 convolution_convert_fusion.1.refs_1_
  121.3 80.5 %shard_map.163 = bf16[2,768,1536]{2,1,0:T(8,128)(2,1)S(1)} custom-call(bf16[768,1536]{1,0:T(8,128)(2,1)S(1)} %convolution_convert_fusion.2.refs_0_, bf16[768,1536]{1,0:T(8,128)(2,1)S(1)} %convolution_convert_fusion.1.refs_1_), custom_call_target="tpu_custom_call" | custom-call | flops 2359296 | bytes 9437184 | tf_op jit(solution)/shard_map/pallas_call | solution.py:306
  201.8 2.1 copy-done.1
  204.0 1.0 fusion.8
  205.0 5.0 %all-reduce = (f32[512]{0:T(512)S(1)}, f32[512]{0:T(512)S(1)}) all-reduce(f32[512]{0:T(512)S(1)} %get-tuple-element.46, f32[512]{0:T(512)S(1)} %get-tuple-element.45), channel_id=1, replica_groups=mesh['dp'=16,'tensor'=2] {'tensor'}, use_global_device_ids=true, to_apply=%region_10.11 | all-reduce | flops 1024 | bytes 8192 | tf_op jit(solution)/shard_map/psum | solution.py:442
  210.0 1.4 convert_element_type.72
  211.4 0.5 copy-done.18
  211.8 1.7 multiply_reduce_fusion
  213.6 2.7 gather_fusion.2
  216.3 4.2 %convolution_convert_fusion.refs_0_ = bf16[768,1536]{1,0:T(8,128)(2,1)} fusion(bf16[512,768]{1,0:T(8,128)(2,1)S(1)} %copy-done.8, bf16[512,1536]{1,0:T(8,128)(2,1)} %copy-done.17), kind=kOutput, calls=%fused_computation.10 | convolution fusion | flops 1209139200 | bytes 4718592 | tf_op jit(solution)/shard_map/dot_general | solution.py:445
  220.5 4.2 %all-to-all-start.1 = ((bf16[16,4,8,768]{3,2,1,0:T(8,128)(2,1)}), bf16[16,4,8,768]{3,2,1,0:T(8,128)(2,1)S(1)}, u32[]{:S(2)}, u32[]{:S(2)}) async-start(bf16[16,4,8,768]{3,2,1,0:T(8,128)(2,1)} %bitcast.60), calls=%async_computation.3 | async-start | bytes 1572864 | tf_op jit(solution)/shard_map/all_to_all | solution.py:488
  225.1 1.7 copy-done.2
  226.7 58.2 %shard_map.164 = (bf16[1,768,1536]{2,1,0:T(8,128)(2,1)S(1)}, f32[34,768]{1,0:T(8,128)S(1)}) custom-call(bf16[768,1536]{1,0:T(8,128)(2,1)S(1)} %copy-done.2, f32[34,768]{1,0:T(8,128)S(1)} %pad_maximum_fusion.refs_1_), custom_call_target="tpu_custom_call" | custom-call | flops 1179648 | bytes 4718592 | tf_op jit(solution)/shard_map/pallas_call | solution.py:306
  284.9 1.4 copy-done.3
  286.3 0.6 slice.17
  286.9 0.6 slice_reduce_fusion
  287.5 2.5 select_convert_fusion
  290.1 1.3 gather_fusion.3
  291.4 5.0 %copy.27 = bf16[2,768,1536]{2,1,0:T(8,128)(2,1)} copy(bf16[2,768,1536]{2,1,0:T(8,128)(2,1)} %copy-done.1) | data formatting | bytes 9437184
  296.4 1.4 copy.28
  (88 shorter events, 1.6 us)
Async XLA Ops:
  7.2 46.8 %copy-start = (bf16[768,1536]{1,0:T(8,128)(2,1)S(1)}, bf16[768,1536]{1,0:T(8,128)(2,1)}, u32[]{:S(2)}) copy-start(bf16[768,1536]{1,0:T(8,128)(2,1)} %param.18) | copy-start | bytes 7077892
  12.9 26.1 %all-to-all-start = ((bf16[16,4,8,768]{3,2,1,0:T(8,128)(2,1)}), bf16[16,4,8,768]{3,2,1,0:T(8,128)(2,1)S(1)}, u32[]{:S(2)}, u32[]{:S(2)}) async-start(bf16[16,4,8,768]{3,2,1,0:T(8,128)(2,1)} %bitcast.62), calls=%async_computation | async-start | bytes 1572864 | tf_op jit(solution)/shard_map/all_to_all | solution.py:392
  20.2 22.6 %copy-start.21 = (f32[768]{0:T(1024)S(1)}, f32[768]{0:T(1024)}, u32[]{:S(2)}) copy-start(f32[768]{0:T(1024)} %param.16) | copy-start | bytes 9220
  20.2 22.6 %copy-start.22 = (f32[768]{0:T(1024)S(1)}, f32[768]{0:T(1024)}, u32[]{:S(2)}) copy-start(f32[768]{0:T(1024)} %param.17) | copy-start | bytes 9220
  20.2 22.8 %copy-start.23 = (s32[512]{0:T(512)S(1)}, s32[512]{0:T(512)}, u32[]{:S(2)}) copy-start(s32[512]{0:T(512)} %param.21) | copy-start | bytes 6148
  20.3 31.0 %all-gather.5.cloned.1.call-start = ((), (), s32[]{:S(2)}) async-start(), calls=%async_computation.5 | async-start | bytes 2359296 | tf_op jit(solution)/shard_map/all_gather | solution.py:388
  21.0 59.6 %all-gather.3.cloned.1.call-start = ((), (), s32[]{:S(2)}) async-start(), calls=%async_computation.4 | async-start | bytes 2359296 | tf_op jit(solution)/shard_map/all_gather | solution.py:405
  38.9 0.9 copy-start.19
  41.5 1.2 copy-start.14
  42.7 167.2 %reduce-scatter.5.cloned.1.call-start = ((), (), s32[]{:S(2)}) async-start(), calls=%async_computation.7 | async-start | bytes 2359296 | tf_op jit(solution)/shard_map/reduce_scatter | solution.py:430
  52.8 1.1 copy-start.17
  80.6 1.9 copy-start.12
  80.6 2.4 copy-start.20
  80.6 2.4 copy-start.24
  82.5 26.1 %slice-start = ((s8[4718592]{0:T(1024)(128)(4,1)}), s8[4194304]{0:T(1024)(128)(4,1)S(1)}, s32[]{:S(2)}) async-start(s8[4718592]{0:T(1024)(128)(4,1)} %bitcast.68), calls=%async_computation.8 | async-start | bytes 8388608
  83.0 5.4 %copy-start.5 = (f32[512,768]{1,0:T(8,128)S(1)}, f32[512,768]{1,0:T(8,128)}, u32[]{:S(2)}) copy-start(f32[512,768]{1,0:T(8,128)} %fusion.27.delta_ref) | copy-start | bytes 4718596
  83.1 5.4 %copy-start.6 = (f32[32,768]{1,0:T(8,128)S(1)}, f32[32,768]{1,0:T(8,128)}, u32[]{:S(2)}) copy-start(f32[32,768]{1,0:T(8,128)} %weight_ref.1) | copy-start | bytes 294916
  83.1 25.5 %slice-start.1 = ((s8[4718592]{0:T(1024)(128)(4,1)}), s8[524288]{0:T(1024)(128)(4,1)S(1)}, s32[]{:S(2)}) async-start(s8[4718592]{0:T(1024)(128)(4,1)} %bitcast.68), calls=%async_computation.9 | async-start | bytes 1048576
  108.5 1.4 copy-start.7
  108.5 1.4 copy-start.11
  108.6 1.4 copy-start.9
  110.0 3.7 %copy-start.8 = (bf16[512,768]{1,0:T(8,128)(2,1)S(1)}, bf16[512,768]{1,0:T(8,128)(2,1)}, u32[]{:S(2)}) copy-start(bf16[512,768]{1,0:T(8,128)(2,1)} %copy-done.7) | copy-start | bytes 2359300
  112.6 175.0 %reduce-scatter.3.cloned.1.call-start = ((), (), s32[]{:S(2)}) async-start(), calls=%async_computation.6 | async-start | bytes 2359296 | tf_op jit(solution)/shard_map/reduce_scatter | solution.py:436
  116.3 3.4 %copy-start.10 = (bf16[512,768]{1,0:T(8,128)(2,1)S(1)}, bf16[512,768]{1,0:T(8,128)(2,1)}, u32[]{:S(2)}) copy-start(bf16[512,768]{1,0:T(8,128)(2,1)} %copy-done.9) | copy-start | bytes 2359300
  116.3 3.4 %copy-start.13 = (bf16[512,1536]{1,0:T(8,128)(2,1)S(1)}, bf16[512,1536]{1,0:T(8,128)(2,1)}, u32[]{:S(2)}) copy-start(bf16[512,1536]{1,0:T(8,128)(2,1)} %all-gather.3.cloned.1.call-done) | copy-start | bytes 4718596
  121.3 82.7 %copy-start.16 = (bf16[512,1536]{1,0:T(8,128)(2,1)S(1)}, bf16[512,1536]{1,0:T(8,128)(2,1)}, u32[]{:S(2)}) copy-start(bf16[512,1536]{1,0:T(8,128)(2,1)} %fusion.9) | copy-start | bytes 4718596
  201.8 2.1 copy-start.1
  210.0 1.4 copy-start.15
  210.0 1.9 copy-start.18
  220.5 69.5 %all-to-all-start.1 = ((bf16[16,4,8,768]{3,2,1,0:T(8,128)(2,1)}), bf16[16,4,8,768]{3,2,1,0:T(8,128)(2,1)S(1)}, u32[]{:S(2)}, u32[]{:S(2)}) async-start(bf16[16,4,8,768]{3,2,1,0:T(8,128)(2,1)} %bitcast.60), calls=%async_computation.3 | async-start | bytes 1572864 | tf_op jit(solution)/shard_map/all_to_all | solution.py:488
  225.0 1.7 copy-start.2
  284.9 1.4 copy-start.3
  291.4 5.0 %copy-start.4 = (bf16[1,768,1536]{2,1,0:T(8,128)(2,1)S(1)}, bf16[1,768,1536]{2,1,0:T(8,128)(2,1)}, u32[]{:S(2)}) copy-start(bf16[1,768,1536]{2,1,0:T(8,128)(2,1)} %copy-done.3) | copy-start | bytes 7077892
Sparse Core Ops, SparseCore 0:
  22.6 28.5 all-gather.4
  53.3 27.2 all-gather.2
  112.7 26.0 reduce-scatter.4
  141.6 26.0 reduce-scatter.2

commit v4 on v3

--- a/solution.py
+++ b/solution.py
@@ -247,40 +247,50 @@
         small_copy(0).start()
     for c in chunks:
         halving(c, 0).start()
-    for s in range(bits):
-        for c in chunks:
-            halving(c, s).wait_recv()
-            kept = held(c, s, digit[orders[c][s]] * lengths[s], lengths[s])
-            come = got.at[c, pl.ds(bases[s], lengths[s])]
-            if s < bits - 1:
-                into = red.at[c, pl.ds(bases[s], lengths[s])]
-            else:
-                into = target(c, offset(c, s), lengths[s])
-
-            @pl.loop(0, lengths[s] // 16)
-            def _(i):
-                rows = pl.ds(pl.multiple_of(i * 16, 16), 16)
-                into[rows, :] = (
-                    kept[rows, :].astype(jnp.float32) + come[rows, :].astype(jnp.float32)
-                ).astype(jnp.bfloat16)
-
-            if s < bits - 1:
-                halving(c, s + 1).start()
-            else:
-                doubling(c, s).start()
-        if with_small:
-            small_copy(s).wait_recv()
-            total = small_buf[s] + small_got[s]
-            if s < bits - 1:
-                small_buf[s + 1] = total
-                small_copy(s + 1).start()
-            else:
-                small_out[...] = total
-    for s in reversed(range(bits)):
-        for c in chunks:
-            doubling(c, s).wait_recv()
-            if s > 0:
-                doubling(c, s - 1).start()
+
+    def halving_done(c, s):
+        halving(c, s).wait_recv()
+        kept = held(c, s, digit[orders[c][s]] * lengths[s], lengths[s])
+        come = got.at[c, pl.ds(bases[s], lengths[s])]
+        if s < bits - 1:
+            into = red.at[c, pl.ds(bases[s], lengths[s])]
+        else:
+            into = target(c, offset(c, s), lengths[s])
+
+        @pl.loop(0, lengths[s] // 16)
+        def _(i):
+            rows = pl.ds(pl.multiple_of(i * 16, 16), 16)
+            into[rows, :] = (
+                kept[rows, :].astype(jnp.float32) + come[rows, :].astype(jnp.float32)
+            ).astype(jnp.bfloat16)
+
+        if s < bits - 1:
+            halving(c, s + 1).start()
+        else:
+            doubling(c, s).start()
+
+    def doubling_done(c, s):
+        doubling(c, s).wait_recv()
+        if s > 0:
+            doubling(c, s - 1).start()
+
+    def small_done(s):
+        small_copy(s).wait_recv()
+        total = small_buf[s] + small_got[s]
+        if s < bits - 1:
+            small_buf[s + 1] = total
+            small_copy(s + 1).start()
+        else:
+            small_out[...] = total
+
+    events = [(c + 2 * k, k, c) for c in chunks for k in range(2 * bits)]
+    for _, k, c in sorted(events):
+        if k < bits:
+            halving_done(c, k)
+            if with_small and c == 0:
+                small_done(k)
+        else:
+            doubling_done(c, 2 * bits - 1 - k)
     for s in range(bits):
         if with_small:
             small_copy(s).wait_send()
@@ -297,7 +307,7 @@
     count = sum(per_array)
     plain = list(range(bits))
     turned = [0] + plain[2:] + [1]
-    orders = [turned if c % 4 == 0 and c + 2 < count else plain for c in range(count)]
+    orders = [turned if c == 0 else plain for c in range(count)]
     vmem = pl.BlockSpec(memory_space=pltpu.VMEM)
     with_small = small is not None
     extra = (small,) if with_small else ()
@@ -318,7 +328,7 @@
         + small_shapes
         + small_semaphores,
         compiler_params=pltpu.CompilerParams(
-            collective_id=collective_id, has_side_effects=True, vmem_limit_bytes=36 * 1024 * 1024
+            collective_id=collective_id, has_side_effects=True, vmem_limit_bytes=44 * 1024 * 1024
         ),
         cost_estimate=pl.CostEstimate(
             flops=count * chunk * width,
@@ -326,6 +336,47 @@
             transcendentals=0,
         ),
     )(*terms, *extra)
+
+
+def exchange_kernel(mine_ref, full_ref, own_sem, send_sem, recv_sem):
+    width = mine_ref.shape[1]
+    me = lax.axis_index("tensor")
+    other = {"tensor": 1 - me}
+    columns = pl.ds(pl.multiple_of(me * width, 128), width)
+    barrier = pltpu.get_barrier_semaphore()
+    pl.semaphore_signal(barrier, inc=1, device_id=other, device_id_type=pl.DeviceIdType.MESH)
+    pl.semaphore_wait(barrier, 1)
+    away = pltpu.make_async_remote_copy(
+        src_ref=mine_ref,
+        dst_ref=full_ref.at[:, columns],
+        send_sem=send_sem,
+        recv_sem=recv_sem,
+        device_id=other,
+        device_id_type=pl.DeviceIdType.MESH,
+    )
+    away.start()
+    own = pltpu.make_async_copy(mine_ref, full_ref.at[:, columns], own_sem)
+    own.start()
+    own.wait()
+    away.wait()
+
+
+def both_halves(mine):
+    rows, width = mine.shape
+    vmem = pl.BlockSpec(memory_space=pltpu.VMEM)
+    return pl.pallas_call(
+        exchange_kernel,
+        out_shape=jax.ShapeDtypeStruct((rows, 2 * width), mine.dtype),
+        in_specs=[vmem],
+        out_specs=vmem,
+        scratch_shapes=[pltpu.SemaphoreType.DMA] * 3,
+        compiler_params=pltpu.CompilerParams(
+            collective_id=3, has_side_effects=True, vmem_limit_bytes=12 * 1024 * 1024
+        ),
+        cost_estimate=pl.CostEstimate(
+            flops=0, bytes_accessed=6 * rows * width, transcendentals=0
+        ),
+    )(mine)
 
 
 def on_device(
@@ -402,7 +453,10 @@
         jnp.zeros((), jnp.bfloat16),
     )
     local_rows = packed.reshape(row_count, part_width)
-    gathered = lax.all_gather(local_rows, "tensor", axis=1, tiled=True)
+    if lax.axis_size("tensor") == 2 and part_width % 128 == 0 and row_count % 64 == 0:
+        gathered = both_halves(local_rows)
+    else:
+        gathered = lax.all_gather(local_rows, "tensor", axis=1, tiled=True)
 
     delta_swish = lax.dot_general(
         delta_whole, output_weight, (((1,), (1,)), ((), ())), preferred_element_type=jnp.float32
@@ -449,16 +503,11 @@
     by_kernel = (
         part_width % (16 * replicas) == 0 and replicas & (replicas - 1) == 0 and replicas > 2
     )
-    terms = (over_rows(delta_linear, normed), over_rows(delta_gate, normed))
-    if by_kernel:
-        terms, mixed_term, swish = lax.optimization_barrier((terms, mixed_term, swish))
-        weight_summed = sum_over_dp(terms, replicas, 1)[0]
-        delta_normed, swish, weight_summed = lax.optimization_barrier(
-            (delta_normed, swish, weight_summed)
-        )
-    else:
-        weight_summed = lax.psum(jnp.stack(terms), "dp")
-    out_term = over_rows(swish, delta_whole)
+    terms = (
+        over_rows(delta_linear, normed),
+        over_rows(delta_gate, normed),
+        over_rows(swish, delta_whole),
+    )
 
     residual_part = lax.dynamic_slice_in_dim(gathered, row_start, rows_part, 0)
     block_output = jnp.where(
@@ -479,12 +528,12 @@
     taps = depth_weight.shape[0]
     norm_local = jnp.stack([jnp.sum(delta_normed * standard, axis=0), jnp.sum(delta_normed, axis=0)])
     small = jnp.concatenate([tap_local, norm_local])
-    homebound, out_term, small = lax.optimization_barrier((homebound, out_term, small))
+    homebound, terms, small = lax.optimization_barrier((homebound, terms, small))
     if by_kernel:
-        out_stack, small_summed = sum_over_dp((out_term,), replicas, 2, small)
-        out_summed = out_stack[0]
+        summed, small_summed = sum_over_dp(terms, replicas, 1, small)
     else:
-        out_summed, small_summed = lax.psum((out_term, small), "dp")
+        summed, small_summed = lax.psum((jnp.stack(terms), small), "dp")
+    weight_summed, out_summed = summed[:2], summed[2]
     returned = lax.all_to_all(homebound, "dp", split_axis=0, concat_axis=0, tiled=True)
     frame_gradient = returned.reshape(replicas * per_peer, BLK, part_width)[pick_back].reshape(
         load_rows, part_width

time: 305 us -> 272 us (0.89)
  waiting for transfers between devices: 49.2 us -> 20.8 us
  Pallas kernels: 159 us -> 151 us
    pallas_call x2 -> x1, Pallas kernels: 139 us -> 106 us  [sum_over_dp(): pl.pallas_call(functools.partial(sum_kernel, chunk, per_array, orders, wi...]
    pallas_call x0 -> x1, Pallas kernels: none -> 24.9 us  [both_halves(): pl.pallas_call(exchange_kernel, out_shape=jax.ShapeDtypeStruct((rows, 2 *...]
    all_gather x1 -> x0, waiting for transfers between devices: 24.1 us -> none  [on_device(): gathered = lax.all_gather(local_rows, 'tensor', axis=1, tiled=True)]
    all_gather x1, waiting for transfers between devices: 8.05 us -> 0.01 us  [on_device(): upstream_whole = lax.all_gather(upstream, 'tensor', axis=0, tiled=True)]
    unnamed x56 -> x48, local copies, waits for them, and re-layouts: 14.2 us -> 7.05 us
    slice x0 -> x1, local copies, waits for them, and re-layouts: none -> 4.82 us  [on_device(): weight_summed, out_summed = (summed[:2], summed[2])]
    reduce_scatter x1, waiting for transfers between devices: 0.01 us -> 4 us  [on_device(): lax.psum_scatter(back_term, 'tensor', scatter_dimension=1, tiled=True)]
    squeeze x0 -> x1, local copies, waits for them, and re-layouts: none -> 3.22 us  [on_device(): weight_summed, out_summed = (summed[:2], summed[2])]
  transfers between devices with their start and end apart: 6 -> 5, of which waited for: 3 -> 2; matrix products, arithmetic and copies ran while one was open for 11% -> 17% of each run, Pallas kernels for 46% -> 48%
where the time goes in v4:
time: 272 us; the launch traced here: 270 us
  Pallas kernels  151 us (56%)
  local copies, waits for them, and re-layouts  27.1 us (10%)
  matrix products  22.7 us (8%)
  waiting for transfers between devices  20.8 us (8%)
  other arithmetic  16.5 us (6%)
  between operations  14.1 us (5%)
  starting transfers between devices  13.1 us (5%)
  blocking collectives  5.17 us (2%)
    pallas_call x1, Pallas kernels, sum_over_dp(): pl.pallas_call(functools.partial(sum_kernel, chunk, per_array, orders, wi...  106 us
    pallas_call x1, Pallas kernels, both_halves(): pl.pallas_call(exchange_kernel, out_shape=jax.ShapeDtypeStruct((rows, 2 *...  24.9 us
    pallas_call x1, Pallas kernels, conv_both(): pl.pallas_call(functools.partial(conv_kernel, taps, taps // 2, tile), gri...  20.1 us
    all_to_all x1, waiting for transfers between devices, on_device(): lax.all_to_all(outbox.reshape(replicas, per_peer, BLK, part_width), 'dp',...  16 us
    dot_general x3, matrix products, over_rows(): lax.dot_general(left, right, (((0,), (0,)), ((), ())), preferred_element_...  10.4 us
    all_to_all x1, starting transfers between devices, on_device(): lax.all_to_all(outbox.reshape(replicas, per_peer, BLK, part_width), 'dp',...  7.4 us
    unnamed x48, local copies, waits for them, and re-layouts  7.05 us
    all_to_all x1, starting transfers between devices, on_device(): lax.all_to_all(homebound, 'dp', split_axis=0, concat_axis=0, tiled=True)  5.62 us
  transfers between devices with their start and end apart: 5, of which 2 were waited for; matrix products, arithmetic and copies ran while one was open for 17% of the time, Pallas kernels for 48%

profile of v4, /device:TPU:0, one launch (start us, length us, event | category | flops | bytes accessed | tf_op | source)
XLA Modules:
  0.0 270.1 jit_solution(399423140486644186)
XLA Ops:
  7.2 0.9 copy.22
  8.1 0.1 reduce
  8.3 1.3 fusion.24
  9.6 0.7 and_select_fusion.1
  10.4 2.5 gather_fusion
  12.9 7.4 %all-to-all-start = ((bf16[16,4,8,768]{3,2,1,0:T(8,128)(2,1)}), bf16[16,4,8,768]{3,2,1,0:T(8,128)(2,1)}, u32[]{:S(2)}, u32[]{:S(2)}) async-start(bf16[16,4,8,768]{3,2,1,0:T(8,128)(2,1)} %bitcast.3), calls=%async_computation | async-start | bytes 1572864 | tf_op jit(solution)/shard_map/all_to_all | solution.py:443
  20.3 0.7 all-gather.2.cloned.1.call-update
  21.1 0.7 iota_compare_fusion.1
  21.9 0.1 reshape.455
  22.0 0.1 convert_element_type.80.active_ref
  22.2 0.1 copy.23.seg_ref
  22.3 0.7 fusion.26
  23.0 16.0 %all-to-all-done = bf16[16,4,8,768]{3,2,1,0:T(8,128)(2,1)} async-done(((bf16[16,4,8,768]{3,2,1,0:T(8,128)(2,1)}), bf16[16,4,8,768]{3,2,1,0:T(8,128)(2,1)}, u32[]{:S(2)}, u32[]{:S(2)}) %all-to-all-start) | async-done | bytes 786464 | tf_op jit(solution)/shard_map/all_to_all | solution.py:443
  39.1 2.6 gather_fusion.1
  41.7 1.3 bitcast_select_fusion.mine_ref
  43.0 24.9 %shard_map.162 = bf16[512,1536]{1,0:T(8,128)(2,1)S(1)} custom-call(bf16[512,768]{1,0:T(8,128)(2,1)S(1)} %bitcast_select_fusion.mine_ref), custom_call_target="tpu_custom_call" | custom-call | bytes 2359296 | tf_op jit(solution)/shard_map/pallas_call | solution.py:367
  67.9 0.3 convert_reduce_fusion
  68.2 0.5 fusion.7
  68.7 0.3 copy-done.1
  69.0 4.4 %convolution_bitcast_fusion.linear_ref.gate_ref = f32[2,512,768]{2,1,0:T(8,128)} fusion(bf16[2,768,1536]{2,1,0:T(8,128)(2,1)S(1)} %copy-done.20, bf16[512,1536]{1,0:T(8,128)(2,1)S(1)} %shard_map.162, f32[1536]{0:T(1024)S(1)} %copy-done.21, f32[1536]{0:T(1024)S(1)} %copy-done.16, f32[512]{0:T(512)S(1)} %add_rsqrt_fusion, f32[512]{0:T(512)S(1)} %broadcast_multiply_fusion.2), kind=kOutput, calls=%fused_computation.31 | convolution fusion | flops 2420637696 | bytes 9453568 | tf_op jit(solution)/shard_map/td,kcd->ktc/dot_general | solution.py:471
  73.4 1.6 broadcast_select_fusion
  75.0 1.2 copy-done.15
  76.2 1.4 fusion.33.delta_ref
  77.6 0.5 copy-done.3
  78.1 20.1 %shard_map.163 = (bf16[512,768]{1,0:T(8,128)(2,1)S(1)}, bf16[512,768]{1,0:T(8,128)(2,1)S(1)}, bf16[512,768]{1,0:T(8,128)(2,1)S(1)}, f32[32,768]{1,0:T(8,128)S(1)}) custom-call(f32[2,512,768]{2,1,0:T(8,128)S(1)} %copy-done.3, f32[2,512,768]{2,1,0:T(8,128)S(1)} %copy-done.3, f32[512,768]{1,0:T(8,128)S(1)} %fusion.33.delta_ref, s32[512,1]{1,0:T(8,128)S(1)} %copy.23.seg_ref, ...), custom_call_target="tpu_custom_call" | custom-call | flops 125829120 | bytes 7077888 | tf_op jit(solution)/shard_map/pallas_call | solution.py:129
  98.2 1.4 fusion.11
  99.6 2.6 fusion.9
  102.3 0.7 subtract_clamp_fusion
  103.3 2.6 convolution_convert_fusion.3
  106.1 2.9 %fusion.8 = (f32[512]{0:T(512)S(1)}, f32[512]{0:T(512)S(1)}) fusion(bf16[512,1536]{1,0:T(8,128)(2,1)} %fusion.9, f32[1536]{0:T(1024)S(1)} %copy-done.16, f32[512]{0:T(512)S(1)} %add_rsqrt_fusion, f32[512]{0:T(512)S(1)} %broadcast_multiply_fusion.2, bf16[512,1536]{1,0:T(8,128)(2,1)} %copy-done.1), kind=kLoop, calls=%fused_computation.19 | loop fusion | flops 6290432 | bytes 3160064 | tf_op jit(solution)/shard_map/reduce_sum | solution.py:494
  109.0 5.2 %all-reduce = (f32[512]{0:T(512)S(1)}, f32[512]{0:T(512)S(1)}) all-reduce(f32[512]{0:T(512)S(1)} %get-tuple-element.38, f32[512]{0:T(512)S(1)} %get-tuple-element.37), channel_id=1, replica_groups=mesh['dp'=16,'tensor'=2] {'tensor'}, use_global_device_ids=true, to_apply=%region_10.11 | all-reduce | flops 1024 | bytes 8192 | tf_op jit(solution)/shard_map/psum | solution.py:496
  114.2 4.4 %convolution_convert_fusion.refs_2_ = bf16[768,1536]{1,0:T(8,128)(2,1)} fusion(bf16[512,768]{1,0:T(8,128)(2,1)S(1)} %copy-done.13, bf16[512,1536]{1,0:T(8,128)(2,1)} %copy-done.15), kind=kOutput, calls=%fused_computation.10 | convolution fusion | flops 1209139200 | bytes 4718592 | tf_op jit(solution)/shard_map/dot_general | solution.py:499
  118.5 3.0 %convolution_convert_fusion.1.refs_1_ = bf16[768,1536]{1,0:T(8,128)(2,1)} fusion(bf16[512,768]{1,0:T(8,128)(2,1)S(1)} %copy-done.11, bf16[512,1536]{1,0:T(8,128)(2,1)S(1)} %copy-done.2, f32[1536]{0:T(1024)S(1)} %copy-done.21, f32[1536]{0:T(1024)S(1)} %copy-done.16, f32[512]{0:T(512)S(1)} %add_rsqrt_fusion, f32[512]{0:T(512)S(1)} %broadcast_multiply_fusion.2), kind=kOutput, calls=%fused_computation.11 | convolution fusion | flops 1213857792 | bytes 4734976 | tf_op jit(solution)/shard_map/dot_general | solution.py:499
  121.5 3.0 %convolution_convert_fusion.2.refs_0_ = bf16[768,1536]{1,0:T(8,128)(2,1)} fusion(bf16[512,768]{1,0:T(8,128)(2,1)S(1)} %copy-done.9, bf16[512,1536]{1,0:T(8,128)(2,1)S(1)} %copy-done.2, f32[1536]{0:T(1024)S(1)} %copy-done.21, f32[1536]{0:T(1024)S(1)} %copy-done.16, f32[512]{0:T(512)S(1)} %add_rsqrt_fusion, f32[512]{0:T(512)S(1)} %broadcast_multiply_fusion.2), kind=kOutput, calls=%fused_computation.12 | convolution fusion | flops 1213857792 | bytes 4734976 | tf_op jit(solution)/shard_map/dot_general | solution.py:499
  124.5 4.0 %reduce-scatter.5.cloned.1.call-done = bf16[512,768]{1,0:T(8,128)(2,1)} async-done(((bf16[512,1536]{1,0:T(8,128)(2,1)}), bf16[512,768]{1,0:T(8,128)(2,1)}) %reduce-scatter.5.cloned.1.call-update) | async-done | bytes 786448 | tf_op jit(solution)/shard_map/reduce_scatter | solution.py:484
  128.5 2.9 %fusion.20 = (f32[768]{0:T(1024)S(1)}, f32[768]{0:T(1024)S(1)}, bf16[64,8,768]{2,1,0:T(8,128)(2,1)}) fusion(bf16[512,768]{1,0:T(8,128)(2,1)} %reduce-scatter.5.cloned.1.call-done, f32[512]{0:T(512)S(1)} %broadcast_multiply_fusion.2, f32[512]{0:T(512)S(1)} %add_rsqrt_fusion, f32[512]{0:T(512)S(1)} %broadcast_multiply_fusion, ...), kind=kLoop, calls=%fused_computation.37 | loop fusion | flops 6289920 | bytes 3163652 | tf_op jit(solution)/shard_map/reduce_sum | solution.py:529
  131.4 2.6 gather_fusion.2
  134.1 5.6 %all-to-all-start.1 = ((bf16[16,4,8,768]{3,2,1,0:T(8,128)(2,1)}), bf16[16,4,8,768]{3,2,1,0:T(8,128)(2,1)S(1)}, u32[]{:S(2)}, u32[]{:S(2)}) async-start(bf16[16,4,8,768]{3,2,1,0:T(8,128)(2,1)} %bitcast.14), calls=%async_computation.3 | async-start | bytes 1572864 | tf_op jit(solution)/shard_map/all_to_all | solution.py:537
  139.7 1.7 copy-done.4
  141.4 1.7 copy-done.5
  143.1 1.7 copy-done.6
  144.7 105.7 %shard_map.164 = (bf16[3,768,1536]{2,1,0:T(8,128)(2,1)}, f32[34,768]{1,0:T(8,128)S(1)}) custom-call(bf16[768,1536]{1,0:T(8,128)(2,1)S(1)} %copy-done.6, bf16[768,1536]{1,0:T(8,128)(2,1)S(1)} %copy-done.5, bf16[768,1536]{1,0:T(8,128)(2,1)S(1)} %copy-done.4, f32[34,768]{1,0:T(8,128)S(1)} %pad_maximum_fusion.refs_3_), custom_call_target="tpu_custom_call" | custom-call | flops 3538944 | bytes 14155776 | tf_op jit(solution)/shard_map/pallas_call | solution.py:316
  250.5 0.6 slice.25
  251.1 4.8 %slice.23 = bf16[2,768,1536]{2,1,0:T(8,128)(2,1)} slice(bf16[3,768,1536]{2,1,0:T(8,128)(2,1)} %get-tuple-element.35), slice={[0:2], [0:768], [0:1536]} | slice | bytes 9437184 | tf_op jit(solution)/shard_map/slice | solution.py:536
  256.0 0.6 slice_reduce_fusion
  256.6 2.5 select_convert_fusion
  259.1 3.2 %slice_bitcast_fusion = bf16[768,1536]{1,0:T(8,128)(2,1)} fusion(bf16[3,768,1536]{2,1,0:T(8,128)(2,1)} %get-tuple-element.35), kind=kLoop, calls=%fused_computation.28 | loop fusion | bytes 4718592 | tf_op jit(solution)/shard_map/squeeze | solution.py:536
  262.3 1.3 gather_fusion.3
  (78 shorter events, 1.1 us)
Async XLA Ops:
  7.2 69.0 %copy-start = (bf16[768,1536]{1,0:T(8,128)(2,1)S(1)}, bf16[768,1536]{1,0:T(8,128)(2,1)}, u32[]{:S(2)}) copy-start(bf16[768,1536]{1,0:T(8,128)(2,1)} %param.18) | copy-start | bytes 7077892
  7.2 13.9 %copy-start.17 = (f32[768]{0:T(1024)S(1)}, f32[768]{0:T(1024)}, u32[]{:S(2)}) copy-start(f32[768]{0:T(1024)} %param.16) | copy-start | bytes 9220
  7.2 13.9 %copy-start.18 = (f32[768]{0:T(1024)S(1)}, f32[768]{0:T(1024)}, u32[]{:S(2)}) copy-start(f32[768]{0:T(1024)} %param.17) | copy-start | bytes 9220
  7.2 15.0 %copy-start.19 = (s32[512]{0:T(512)S(1)}, s32[512]{0:T(512)}, u32[]{:S(2)}) copy-start(s32[512]{0:T(512)} %param.21) | copy-start | bytes 6148
  12.9 26.2 %all-to-all-start = ((bf16[16,4,8,768]{3,2,1,0:T(8,128)(2,1)}), bf16[16,4,8,768]{3,2,1,0:T(8,128)(2,1)}, u32[]{:S(2)}, u32[]{:S(2)}) async-start(bf16[16,4,8,768]{3,2,1,0:T(8,128)(2,1)} %bitcast.3), calls=%async_computation | async-start | bytes 1572864 | tf_op jit(solution)/shard_map/all_to_all | solution.py:443
  20.3 53.1 %all-gather.2.cloned.1.call-start = ((), (), s32[]{:S(2)}) async-start(), calls=%async_computation.4 | async-start | bytes 2359296 | tf_op jit(solution)/shard_map/all_gather | solution.py:439
  21.0 107.5 %reduce-scatter.5.cloned.1.call-start = ((), (), s32[]{:S(2)}) async-start(), calls=%async_computation.6 | async-start | bytes 2359296 | tf_op jit(solution)/shard_map/reduce_scatter | solution.py:484
  42.9 26.1 %copy-start.16 = (f32[1536]{0:T(1024)S(1)}, f32[1536]{0:T(1024)}, u32[]{:S(2)}) copy-start(f32[1536]{0:T(1024)} %param.12) | copy-start | bytes 18436
  43.0 26.1 %copy-start.20 = (bf16[2,768,1536]{2,1,0:T(8,128)(2,1)S(1)}, bf16[2,768,1536]{2,1,0:T(8,128)(2,1)}, u32[]{:S(2)}) copy-start(bf16[2,768,1536]{2,1,0:T(8,128)(2,1)} %param.14) | copy-start | bytes 14155780
  43.0 26.1 %copy-start.21 = (f32[1536]{0:T(1024)S(1)}, f32[1536]{0:T(1024)}, u32[]{:S(2)}) copy-start(f32[1536]{0:T(1024)} %param.13) | copy-start | bytes 18436
  67.9 1.2 copy-start.1
  75.0 1.2 copy-start.15
  76.2 1.9 copy-start.3
  76.2 1.9 copy-start.7
  76.2 22.0 %slice-start = ((s8[4718592]{0:T(1024)(128)(4,1)}), s8[4194304]{0:T(1024)(128)(4,1)S(1)}, s32[]{:S(2)}) async-start(s8[4718592]{0:T(1024)(128)(4,1)} %bitcast.65), calls=%async_computation.7 | async-start | bytes 8388608
  78.1 20.1 %slice-start.1 = ((s8[4718592]{0:T(1024)(128)(4,1)}), s8[524288]{0:T(1024)(128)(4,1)S(1)}, s32[]{:S(2)}) async-start(s8[4718592]{0:T(1024)(128)(4,1)} %bitcast.65), calls=%async_computation.8 | async-start | bytes 1048576
  98.1 1.5 copy-start.8
  98.1 1.5 copy-start.12
  98.2 1.4 copy-start.10
  99.6 3.6 %copy-start.13 = (bf16[512,768]{1,0:T(8,128)(2,1)S(1)}, bf16[512,768]{1,0:T(8,128)(2,1)}, u32[]{:S(2)}) copy-start(bf16[512,768]{1,0:T(8,128)(2,1)} %copy-done.12) | copy-start | bytes 2359300
  102.2 154.4 %reduce-scatter.3.cloned.1.call-start = ((), (), s32[]{:S(2)}) async-start(), calls=%async_computation.5 | async-start | bytes 2359296 | tf_op jit(solution)/shard_map/reduce_scatter | solution.py:490
  114.1 4.4 %copy-start.2 = (bf16[512,1536]{1,0:T(8,128)(2,1)S(1)}, bf16[512,1536]{1,0:T(8,128)(2,1)}, u32[]{:S(2)}) copy-start(bf16[512,1536]{1,0:T(8,128)(2,1)} %copy-done.1) | copy-start | bytes 4718596
  114.1 4.4 %copy-start.11 = (bf16[512,768]{1,0:T(8,128)(2,1)S(1)}, bf16[512,768]{1,0:T(8,128)(2,1)}, u32[]{:S(2)}) copy-start(bf16[512,768]{1,0:T(8,128)(2,1)} %copy-done.10) | copy-start | bytes 2359300
  118.5 3.0 %copy-start.9 = (bf16[512,768]{1,0:T(8,128)(2,1)S(1)}, bf16[512,768]{1,0:T(8,128)(2,1)}, u32[]{:S(2)}) copy-start(bf16[512,768]{1,0:T(8,128)(2,1)} %copy-done.8) | copy-start | bytes 2359300
  121.5 7.0 %copy-start.14 = (bf16[64,8,768]{2,1,0:T(8,128)(2,1)S(1)}, bf16[64,8,768]{2,1,0:T(8,128)(2,1)}, u32[]{:S(2)}) copy-start(bf16[64,8,768]{2,1,0:T(8,128)(2,1)} %gather_fusion.1) | copy-start | bytes 2359300
  134.1 128.2 %all-to-all-start.1 = ((bf16[16,4,8,768]{3,2,1,0:T(8,128)(2,1)}), bf16[16,4,8,768]{3,2,1,0:T(8,128)(2,1)S(1)}, u32[]{:S(2)}, u32[]{:S(2)}) async-start(bf16[16,4,8,768]{3,2,1,0:T(8,128)(2,1)} %bitcast.14), calls=%async_computation.3 | async-start | bytes 1572864 | tf_op jit(solution)/shard_map/all_to_all | solution.py:537
  139.7 1.7 copy-start.4
  141.4 1.7 copy-start.5
  143.1 1.7 copy-start.6
Sparse Core Ops, SparseCore 0:
  22.7 33.6 all-gather.1
  102.3 26.1 reduce-scatter.4
  130.9 26.0 reduce-scatter.2

commit v5 on v4

--- a/solution.py
+++ b/solution.py
@@ -176,10 +176,11 @@
     bits = len(orders[0])
     ins, refs = refs[:arrays], refs[arrays:]
     if with_small:
-        small_in, stacked_out, small_out, red, got, sends, recvs = refs[:7]
-        small_buf, small_got, small_sends, small_recvs = refs[7:]
+        small_in, stacked_out, last_out, small_out = refs[:4]
+        red, got, first, loads, sends, recvs = refs[4:10]
+        small_buf, small_got, small_sends, small_recvs = refs[10:]
     else:
-        stacked_out, red, got, sends, recvs = refs
+        stacked_out, last_out, red, got, first, loads, sends, recvs = refs
     me = lax.axis_index("dp")
     digit = [(me // (1 << b)) % 2 for b in range(bits)]
     partner = [me + (1 - 2 * digit[b]) * (1 << b) for b in range(bits)]
@@ -189,14 +190,14 @@
     bases = [chunk - 2 * lengths[s] for s in range(bits)]
 
     def target(c, start, size):
-        a, first = places[c]
-        rows = pl.ds(pl.multiple_of(first + start, 16), size)
-        return stacked_out.at[a, rows]
+        a, top = places[c]
+        rows = pl.ds(pl.multiple_of(top + start, 16), size)
+        return stacked_out.at[a, rows] if a < arrays - 1 else last_out.at[rows]
 
     def held(c, s, start, size):
         if s == 0:
-            a, first = places[c]
-            return ins[a].at[pl.ds(pl.multiple_of(first + start, 16), size)]
+            a, top = places[c]
+            return ins[a].at[pl.ds(pl.multiple_of(top + start, 16), size)]
         return red.at[c, pl.ds(pl.multiple_of(bases[s - 1] + start, 16), size)]
 
     def halving(c, s):
@@ -208,6 +209,12 @@
             recv_sem=recvs.at[s, c],
             device_id={"dp": partner[b]},
             device_id_type=pl.DeviceIdType.MESH,
+        )
+
+    def load(c):
+        b = orders[c][0]
+        return pltpu.make_async_copy(
+            held(c, 0, digit[b] * lengths[0], lengths[0]), first.at[c], loads.at[c]
         )
 
     def offset(c, s):
@@ -247,10 +254,16 @@
         small_copy(0).start()
     for c in chunks:
         halving(c, 0).start()
+    for c in chunks:
+        load(c).start()
 
     def halving_done(c, s):
         halving(c, s).wait_recv()
-        kept = held(c, s, digit[orders[c][s]] * lengths[s], lengths[s])
+        if s == 0:
+            load(c).wait()
+            kept = first.at[c]
+        else:
+            kept = held(c, s, digit[orders[c][s]] * lengths[s], lengths[s])
         come = got.at[c, pl.ds(bases[s], lengths[s])]
         if s < bits - 1:
             into = red.at[c, pl.ds(bases[s], lengths[s])]
@@ -315,13 +328,18 @@
     small_semaphores = [pltpu.SemaphoreType.DMA((bits,)) for e in extra * 2]
     return pl.pallas_call(
         functools.partial(sum_kernel, chunk, per_array, orders, with_small),
-        out_shape=[jax.ShapeDtypeStruct((len(terms), rows, width), jnp.bfloat16)]
+        out_shape=[
+            jax.ShapeDtypeStruct((len(terms) - 1, rows, width), jnp.bfloat16),
+            jax.ShapeDtypeStruct((rows, width), jnp.bfloat16),
+        ]
         + [jax.ShapeDtypeStruct(e.shape, jnp.float32) for e in extra],
-        in_specs=[vmem] * (len(terms) + len(extra)),
-        out_specs=[vmem] * (1 + len(extra)),
+        in_specs=[pl.BlockSpec(memory_space=pl.ANY)] * len(terms) + [vmem] * len(extra),
+        out_specs=[vmem] * (2 + len(extra)),
         scratch_shapes=[
             pltpu.VMEM((count, chunk, width), jnp.bfloat16),
             pltpu.VMEM((count, chunk, width), jnp.bfloat16),
+            pltpu.VMEM((count, chunk // 2, width), jnp.bfloat16),
+            pltpu.SemaphoreType.DMA((count,)),
             pltpu.SemaphoreType.DMA((2 * bits, count)),
             pltpu.SemaphoreType.DMA((2 * bits, count)),
         ]
@@ -530,10 +548,11 @@
     small = jnp.concatenate([tap_local, norm_local])
     homebound, terms, small = lax.optimization_barrier((homebound, terms, small))
     if by_kernel:
-        summed, small_summed = sum_over_dp(terms, replicas, 1, small)
+        weight_summed, out_summed, small_summed = sum_over_dp(terms, replicas, 1, small)
     else:
-        summed, small_summed = lax.psum((jnp.stack(terms), small), "dp")
-    weight_summed, out_summed = summed[:2], summed[2]
+        weight_summed, out_summed, small_summed = lax.psum(
+            (jnp.stack(terms[:2]), terms[2], small), "dp"
+        )
     returned = lax.all_to_all(homebound, "dp", split_axis=0, concat_axis=0, tiled=True)
     frame_gradient = returned.reshape(replicas * per_peer, BLK, part_width)[pick_back].reshape(
         load_rows, part_width

time: 272 us -> 270 us (level)
    unnamed x48 -> x54, local copies, waits for them, and re-layouts: 7.05 us -> 14.8 us
    slice x1 -> x0, local copies, waits for them, and re-layouts: 4.82 us -> none  [on_device(): weight_summed, out_summed = (summed[:2], summed[2])]
    squeeze x1 -> x0, local copies, waits for them, and re-layouts: 3.22 us -> none  [on_device(): weight_summed, out_summed = (summed[:2], summed[2])]
  transfers between devices with their start and end apart: 5 -> 5, of which waited for: 2 -> 2; matrix products, arithmetic and copies ran while one was open for 17% -> 14% of each run, Pallas kernels for 48% -> 48%
where the time goes in v5:
time: 270 us; the launch traced here: 269 us
  Pallas kernels  149 us (55%)
  local copies, waits for them, and re-layouts  26.9 us (10%)
  matrix products  22.7 us (8%)
  waiting for transfers between devices  21.1 us (8%)
  other arithmetic  16.5 us (6%)
  between operations  14.2 us (5%)
  starting transfers between devices  13.1 us (5%)
  blocking collectives  5.17 us (2%)
    pallas_call x1, Pallas kernels, sum_over_dp(): pl.pallas_call(functools.partial(sum_kernel, chunk, per_array, orders, wi...  105 us
    pallas_call x1, Pallas kernels, both_halves(): pl.pallas_call(exchange_kernel, out_shape=jax.ShapeDtypeStruct((rows, 2 *...  24.9 us
    pallas_call x1, Pallas kernels, conv_both(): pl.pallas_call(functools.partial(conv_kernel, taps, taps // 2, tile), gri...  20.1 us
    all_to_all x1, waiting for transfers between devices, on_device(): lax.all_to_all(outbox.reshape(replicas, per_peer, BLK, part_width), 'dp',...  16 us
    unnamed x54, local copies, waits for them, and re-layouts  14.8 us
    dot_general x3, matrix products, over_rows(): lax.dot_general(left, right, (((0,), (0,)), ((), ())), preferred_element_...  10.4 us
    all_to_all x1, starting transfers between devices, on_device(): lax.all_to_all(outbox.reshape(replicas, per_peer, BLK, part_width), 'dp',...  7.4 us
    all_to_all x1, starting transfers between devices, on_device(): lax.all_to_all(homebound, 'dp', split_axis=0, concat_axis=0, tiled=True)  5.62 us
  transfers between devices with their start and end apart: 5, of which 2 were waited for; matrix products, arithmetic and copies ran while one was open for 14% of the time, Pallas kernels for 48%

profile of v5, /device:TPU:0, one launch (start us, length us, event | category | flops | bytes accessed | tf_op | source)
XLA Modules:
  0.0 269.1 jit_solution(13754261214676254312)
XLA Ops:
  7.2 0.9 copy.22
  8.1 0.1 reduce
  8.3 1.3 fusion.24
  9.6 0.7 and_select_fusion.1
  10.4 2.5 gather_fusion
  12.9 7.4 %all-to-all-start = ((bf16[16,4,8,768]{3,2,1,0:T(8,128)(2,1)}), bf16[16,4,8,768]{3,2,1,0:T(8,128)(2,1)}, u32[]{:S(2)}, u32[]{:S(2)}) async-start(bf16[16,4,8,768]{3,2,1,0:T(8,128)(2,1)} %bitcast.3), calls=%async_computation | async-start | bytes 1572864 | tf_op jit(solution)/shard_map/all_to_all | solution.py:461
  20.3 0.7 all-gather.2.cloned.1.call-update
  21.1 0.7 iota_compare_fusion.1
  22.0 0.1 convert_element_type.80.active_ref
  22.2 0.1 copy.23.seg_ref
  22.3 0.7 fusion.26
  23.0 16.0 %all-to-all-done = bf16[16,4,8,768]{3,2,1,0:T(8,128)(2,1)} async-done(((bf16[16,4,8,768]{3,2,1,0:T(8,128)(2,1)}), bf16[16,4,8,768]{3,2,1,0:T(8,128)(2,1)}, u32[]{:S(2)}, u32[]{:S(2)}) %all-to-all-start) | async-done | bytes 786464 | tf_op jit(solution)/shard_map/all_to_all | solution.py:461
  39.1 2.6 gather_fusion.1
  41.7 1.3 bitcast_select_fusion.mine_ref
  43.0 24.9 %shard_map.162 = bf16[512,1536]{1,0:T(8,128)(2,1)S(1)} custom-call(bf16[512,768]{1,0:T(8,128)(2,1)S(1)} %bitcast_select_fusion.mine_ref), custom_call_target="tpu_custom_call" | custom-call | bytes 2359296 | tf_op jit(solution)/shard_map/pallas_call | solution.py:385
  67.9 0.3 convert_reduce_fusion
  68.2 0.5 fusion.7
  68.7 0.3 copy-done.1
  69.0 4.4 %convolution_bitcast_fusion.linear_ref.gate_ref = f32[2,512,768]{2,1,0:T(8,128)} fusion(bf16[2,768,1536]{2,1,0:T(8,128)(2,1)S(1)} %copy-done.22, bf16[512,1536]{1,0:T(8,128)(2,1)S(1)} %shard_map.162, f32[1536]{0:T(1024)S(1)} %copy-done.23, f32[1536]{0:T(1024)S(1)} %copy-done.18, f32[512]{0:T(512)S(1)} %add_rsqrt_fusion, f32[512]{0:T(512)S(1)} %broadcast_multiply_fusion.2), kind=kOutput, calls=%fused_computation.30 | convolution fusion | flops 2420637696 | bytes 9453568 | tf_op jit(solution)/shard_map/td,kcd->ktc/dot_general | solution.py:489
  73.4 1.6 broadcast_select_fusion
  75.0 1.2 copy-done.17
  76.2 1.4 fusion.33.delta_ref
  77.6 0.5 copy-done.3
  78.1 20.1 %shard_map.163 = (bf16[512,768]{1,0:T(8,128)(2,1)S(1)}, bf16[512,768]{1,0:T(8,128)(2,1)S(1)}, bf16[512,768]{1,0:T(8,128)(2,1)S(1)}, f32[32,768]{1,0:T(8,128)S(1)}) custom-call(f32[2,512,768]{2,1,0:T(8,128)S(1)} %copy-done.3, f32[2,512,768]{2,1,0:T(8,128)S(1)} %copy-done.3, f32[512,768]{1,0:T(8,128)S(1)} %fusion.33.delta_ref, s32[512,1]{1,0:T(8,128)S(1)} %copy.23.seg_ref, ...), custom_call_target="tpu_custom_call" | custom-call | flops 125829120 | bytes 7077888 | tf_op jit(solution)/shard_map/pallas_call | solution.py:129
  98.2 1.4 fusion.11
  99.6 2.6 fusion.9
  102.4 0.7 subtract_clamp_fusion
  103.2 2.5 convolution_convert_fusion.3
  105.8 2.9 %fusion.8 = (f32[512]{0:T(512)S(1)}, f32[512]{0:T(512)S(1)}) fusion(bf16[512,1536]{1,0:T(8,128)(2,1)} %fusion.9, f32[1536]{0:T(1024)S(1)} %copy-done.18, f32[512]{0:T(512)S(1)} %add_rsqrt_fusion, f32[512]{0:T(512)S(1)} %broadcast_multiply_fusion.2, bf16[512,1536]{1,0:T(8,128)(2,1)} %copy-done.1), kind=kLoop, calls=%fused_computation.19 | loop fusion | flops 6290432 | bytes 3160064 | tf_op jit(solution)/shard_map/reduce_sum | solution.py:512
  108.7 5.2 %all-reduce = (f32[512]{0:T(512)S(1)}, f32[512]{0:T(512)S(1)}) all-reduce(f32[512]{0:T(512)S(1)} %get-tuple-element.40, f32[512]{0:T(512)S(1)} %get-tuple-element.39), channel_id=1, replica_groups=mesh['dp'=16,'tensor'=2] {'tensor'}, use_global_device_ids=true, to_apply=%region_10.11 | all-reduce | flops 1024 | bytes 8192 | tf_op jit(solution)/shard_map/psum | solution.py:514
  113.9 4.4 %convolution_convert_fusion.refs_2_ = bf16[768,1536]{1,0:T(8,128)(2,1)} fusion(bf16[512,768]{1,0:T(8,128)(2,1)S(1)} %copy-done.15, bf16[512,1536]{1,0:T(8,128)(2,1)} %copy-done.17), kind=kOutput, calls=%fused_computation.10 | convolution fusion | flops 1209139200 | bytes 4718592 | tf_op jit(solution)/shard_map/dot_general | solution.py:517
  118.3 3.0 %convolution_convert_fusion.1.refs_1_ = bf16[768,1536]{1,0:T(8,128)(2,1)} fusion(bf16[512,768]{1,0:T(8,128)(2,1)S(1)} %copy-done.13, bf16[512,1536]{1,0:T(8,128)(2,1)S(1)} %copy-done.2, f32[1536]{0:T(1024)S(1)} %copy-done.23, f32[1536]{0:T(1024)S(1)} %copy-done.18, f32[512]{0:T(512)S(1)} %add_rsqrt_fusion, f32[512]{0:T(512)S(1)} %broadcast_multiply_fusion.2), kind=kOutput, calls=%fused_computation.11 | convolution fusion | flops 1213857792 | bytes 4734976 | tf_op jit(solution)/shard_map/dot_general | solution.py:517
  121.3 3.0 %convolution_convert_fusion.2.refs_0_ = bf16[768,1536]{1,0:T(8,128)(2,1)} fusion(bf16[512,768]{1,0:T(8,128)(2,1)S(1)} %copy-done.11, bf16[512,1536]{1,0:T(8,128)(2,1)S(1)} %copy-done.2, f32[1536]{0:T(1024)S(1)} %copy-done.23, f32[1536]{0:T(1024)S(1)} %copy-done.18, f32[512]{0:T(512)S(1)} %add_rsqrt_fusion, f32[512]{0:T(512)S(1)} %broadcast_multiply_fusion.2), kind=kOutput, calls=%fused_computation.12 | convolution fusion | flops 1213857792 | bytes 4734976 | tf_op jit(solution)/shard_map/dot_general | solution.py:517
  124.3 4.3 %reduce-scatter.5.cloned.1.call-done = bf16[512,768]{1,0:T(8,128)(2,1)} async-done(((bf16[512,1536]{1,0:T(8,128)(2,1)}), bf16[512,768]{1,0:T(8,128)(2,1)}) %reduce-scatter.5.cloned.1.call-update) | async-done | bytes 786448 | tf_op jit(solution)/shard_map/reduce_scatter | solution.py:502
  128.6 2.9 %fusion.20 = (f32[768]{0:T(1024)S(1)}, f32[768]{0:T(1024)S(1)}, bf16[64,8,768]{2,1,0:T(8,128)(2,1)}) fusion(bf16[512,768]{1,0:T(8,128)(2,1)} %reduce-scatter.5.cloned.1.call-done, f32[512]{0:T(512)S(1)} %broadcast_multiply_fusion.2, f32[512]{0:T(512)S(1)} %add_rsqrt_fusion, f32[512]{0:T(512)S(1)} %broadcast_multiply_fusion, ...), kind=kLoop, calls=%fused_computation.36 | loop fusion | flops 6289920 | bytes 3163652 | tf_op jit(solution)/shard_map/reduce_sum | solution.py:547
  131.5 2.7 gather_fusion.2
  134.2 5.6 %all-to-all-start.1 = ((bf16[16,4,8,768]{3,2,1,0:T(8,128)(2,1)}), bf16[16,4,8,768]{3,2,1,0:T(8,128)(2,1)S(1)}, u32[]{:S(2)}, u32[]{:S(2)}) async-start(bf16[16,4,8,768]{3,2,1,0:T(8,128)(2,1)} %bitcast.14), calls=%async_computation.3 | async-start | bytes 1572864 | tf_op jit(solution)/shard_map/all_to_all | solution.py:556
  140.1 1.7 copy-done.6
  141.8 1.7 copy-done.7
  143.4 1.7 copy-done.8
  145.1 104.5 %shard_map.164 = (bf16[2,768,1536]{2,1,0:T(8,128)(2,1)}, bf16[768,1536]{1,0:T(8,128)(2,1)S(1)}, f32[34,768]{1,0:T(8,128)S(1)}) custom-call(bf16[768,1536]{1,0:T(8,128)(2,1)S(1)} %copy-done.8, bf16[768,1536]{1,0:T(8,128)(2,1)S(1)} %copy-done.7, bf16[768,1536]{1,0:T(8,128)(2,1)S(1)} %copy-done.6, f32[34,768]{1,0:T(8,128)S(1)} %pad_maximum_fusion.refs_3_), custom_call_target="tpu_custom_call" | custom-call | flops 3538944 | bytes 14155776 | tf_op jit(solution)/shard_map/pallas_call | solution.py:329
  249.7 1.4 copy-done.4
  251.1 0.6 slice.17
  251.7 0.6 slice_reduce_fusion
  252.4 2.5 select_convert_fusion
  254.9 1.3 gather_fusion.3
  256.2 5.0 %copy.27 = bf16[2,768,1536]{2,1,0:T(8,128)(2,1)} copy(bf16[2,768,1536]{2,1,0:T(8,128)(2,1)} %get-tuple-element.64) | data formatting | bytes 9437184
  261.2 1.4 copy.28
  (82 shorter events, 1.3 us)
Async XLA Ops:
  7.2 69.0 %copy-start = (bf16[768,1536]{1,0:T(8,128)(2,1)S(1)}, bf16[768,1536]{1,0:T(8,128)(2,1)}, u32[]{:S(2)}) copy-start(bf16[768,1536]{1,0:T(8,128)(2,1)} %param.18) | copy-start | bytes 7077892
  7.2 13.9 %copy-start.19 = (f32[768]{0:T(1024)S(1)}, f32[768]{0:T(1024)}, u32[]{:S(2)}) copy-start(f32[768]{0:T(1024)} %param.16) | copy-start | bytes 9220
  7.2 13.9 %copy-start.20 = (f32[768]{0:T(1024)S(1)}, f32[768]{0:T(1024)}, u32[]{:S(2)}) copy-start(f32[768]{0:T(1024)} %param.17) | copy-start | bytes 9220
  7.2 15.0 %copy-start.21 = (s32[512]{0:T(512)S(1)}, s32[512]{0:T(512)}, u32[]{:S(2)}) copy-start(s32[512]{0:T(512)} %param.21) | copy-start | bytes 6148
  12.9 26.2 %all-to-all-start = ((bf16[16,4,8,768]{3,2,1,0:T(8,128)(2,1)}), bf16[16,4,8,768]{3,2,1,0:T(8,128)(2,1)}, u32[]{:S(2)}, u32[]{:S(2)}) async-start(bf16[16,4,8,768]{3,2,1,0:T(8,128)(2,1)} %bitcast.3), calls=%async_computation | async-start | bytes 1572864 | tf_op jit(solution)/shard_map/all_to_all | solution.py:461
  20.3 53.1 %all-gather.2.cloned.1.call-start = ((), (), s32[]{:S(2)}) async-start(), calls=%async_computation.4 | async-start | bytes 2359296 | tf_op jit(solution)/shard_map/all_gather | solution.py:457
  21.0 107.6 %reduce-scatter.5.cloned.1.call-start = ((), (), s32[]{:S(2)}) async-start(), calls=%async_computation.6 | async-start | bytes 2359296 | tf_op jit(solution)/shard_map/reduce_scatter | solution.py:502
  42.9 26.1 %copy-start.18 = (f32[1536]{0:T(1024)S(1)}, f32[1536]{0:T(1024)}, u32[]{:S(2)}) copy-start(f32[1536]{0:T(1024)} %param.12) | copy-start | bytes 18436
  43.0 26.1 %copy-start.22 = (bf16[2,768,1536]{2,1,0:T(8,128)(2,1)S(1)}, bf16[2,768,1536]{2,1,0:T(8,128)(2,1)}, u32[]{:S(2)}) copy-start(bf16[2,768,1536]{2,1,0:T(8,128)(2,1)} %param.14) | copy-start | bytes 14155780
  43.0 26.1 %copy-start.23 = (f32[1536]{0:T(1024)S(1)}, f32[1536]{0:T(1024)}, u32[]{:S(2)}) copy-start(f32[1536]{0:T(1024)} %param.13) | copy-start | bytes 18436
  67.9 1.2 copy-start.1
  75.0 1.2 copy-start.17
  76.2 1.9 copy-start.3
  76.2 1.9 copy-start.9
  76.2 22.0 %slice-start = ((s8[4718592]{0:T(1024)(128)(4,1)}), s8[4194304]{0:T(1024)(128)(4,1)S(1)}, s32[]{:S(2)}) async-start(s8[4718592]{0:T(1024)(128)(4,1)} %bitcast.63), calls=%async_computation.7 | async-start | bytes 8388608
  78.1 20.1 %slice-start.1 = ((s8[4718592]{0:T(1024)(128)(4,1)}), s8[524288]{0:T(1024)(128)(4,1)S(1)}, s32[]{:S(2)}) async-start(s8[4718592]{0:T(1024)(128)(4,1)} %bitcast.63), calls=%async_computation.8 | async-start | bytes 1048576
  98.1 1.5 copy-start.10
  98.1 1.5 copy-start.14
  98.1 1.5 copy-start.12
  99.6 3.6 %copy-start.15 = (bf16[512,768]{1,0:T(8,128)(2,1)S(1)}, bf16[512,768]{1,0:T(8,128)(2,1)}, u32[]{:S(2)}) copy-start(bf16[512,768]{1,0:T(8,128)(2,1)} %copy-done.14) | copy-start | bytes 2359300
  102.3 150.1 %reduce-scatter.3.cloned.1.call-start = ((), (), s32[]{:S(2)}) async-start(), calls=%async_computation.5 | async-start | bytes 2359296 | tf_op jit(solution)/shard_map/reduce_scatter | solution.py:508
  113.9 4.4 %copy-start.2 = (bf16[512,1536]{1,0:T(8,128)(2,1)S(1)}, bf16[512,1536]{1,0:T(8,128)(2,1)}, u32[]{:S(2)}) copy-start(bf16[512,1536]{1,0:T(8,128)(2,1)} %copy-done.1) | copy-start | bytes 4718596
  113.9 4.4 %copy-start.13 = (bf16[512,768]{1,0:T(8,128)(2,1)S(1)}, bf16[512,768]{1,0:T(8,128)(2,1)}, u32[]{:S(2)}) copy-start(bf16[512,768]{1,0:T(8,128)(2,1)} %copy-done.12) | copy-start | bytes 2359300
  118.3 3.0 %copy-start.11 = (bf16[512,768]{1,0:T(8,128)(2,1)S(1)}, bf16[512,768]{1,0:T(8,128)(2,1)}, u32[]{:S(2)}) copy-start(bf16[512,768]{1,0:T(8,128)(2,1)} %copy-done.10) | copy-start | bytes 2359300
  121.3 7.3 %copy-start.16 = (bf16[64,8,768]{2,1,0:T(8,128)(2,1)S(1)}, bf16[64,8,768]{2,1,0:T(8,128)(2,1)}, u32[]{:S(2)}) copy-start(bf16[64,8,768]{2,1,0:T(8,128)(2,1)} %gather_fusion.1) | copy-start | bytes 2359300
  134.2 120.7 %all-to-all-start.1 = ((bf16[16,4,8,768]{3,2,1,0:T(8,128)(2,1)}), bf16[16,4,8,768]{3,2,1,0:T(8,128)(2,1)S(1)}, u32[]{:S(2)}, u32[]{:S(2)}) async-start(bf16[16,4,8,768]{3,2,1,0:T(8,128)(2,1)} %bitcast.14), calls=%async_computation.3 | async-start | bytes 1572864 | tf_op jit(solution)/shard_map/all_to_all | solution.py:556
  140.1 1.7 copy-start.6
  141.8 1.7 copy-start.7
  143.4 1.7 copy-start.8
  249.7 1.4 copy-start.4
  256.2 5.0 %copy-start.5 = (bf16[768,1536]{1,0:T(8,128)(2,1)S(1)}, bf16[768,1536]{1,0:T(8,128)(2,1)}, u32[]{:S(2)}) copy-start(bf16[768,1536]{1,0:T(8,128)(2,1)} %copy-done.4) | copy-start | bytes 7077892
Sparse Core Ops, SparseCore 0:
  22.7 33.6 all-gather.1
  102.4 26.1 reduce-scatter.4
  130.9 26.0 reduce-scatter.2
